TPU v7x, 512 devices: a whole 4x4x16 slice. The times are simulated.
512 devices in a mesh: seq: 64 (over y, z), ch: 8 (over x, core).
Axes of the slice: x: 4, y: 4, z: 16, core: 2. Of those that a mesh axis runs over, the one named last changes fastest.
Arguments:
- gate_query: bfloat16 [2048, 8192], P('ch', 'seq'), may hold values from -6 to 6
- gate_key: bfloat16 [2048, 8192], P('ch', 'seq'), may hold values from -6 to 6
- gate_value: bfloat16 [2048, 8192], P('ch', 'seq'), may hold values from -6 to 6
- filters: float32 [128, 8192], P(None, ('seq', 'ch')), may hold values from -6 to 6
- upstream: bfloat16 [2048, 8192], P('ch', 'seq'), may hold values from -6 to 6
Outputs:
- mixed: bfloat16 [2048, 8192], P('ch', 'seq')
- grad_query: bfloat16 [2048, 8192], P('ch', 'seq')
- grad_key: bfloat16 [2048, 8192], P('ch', 'seq')
- grad_value: bfloat16 [2048, 8192], P('ch', 'seq')
- grad_filters: float32 [128, 8192], P(None, ('seq', 'ch'))
All inputs are finite; a program needn't handle non-finite values.
Results may differ from a plain program's by a relative error of at most 0.002.
Values sent between devices are 32-bit elements; how exact they have to be, the bound alone decides.
No kernel may reach another device: no remote copies, remote signals or barrier semaphores. Data moves between devices by JAX's collectives and lax.ppermute only.
A program may use at most 64 MiB of HBM per device.

v0:
```python
import math

import jax
import jax.numpy as jnp
from jax import lax
from jax.sharding import PartitionSpec as P

lane_width = 128
highest = lax.Precision.HIGHEST


def partner_2(value, axis, stride):
    mask = 2**stride
    pairs = [(source, source ^ mask) for source in range(lax.axis_size(axis))]
    return lax.ppermute(value, axis, pairs)


def dft_table(order_size, sign):
    indices = jnp.arange(order_size, dtype=jnp.int32)
    product = indices[:, None] * indices[None, :] % order_size
    phase_angle = sign * 2.0 * math.pi / order_size * product.astype(jnp.float32)
    return (jnp.cos(phase_angle), jnp.sin(phase_angle))


def cross_table(size_a, size_b, sign):
    first_axis = jnp.arange(size_a, dtype=jnp.int32)[:, None]
    second = jnp.arange(size_b, dtype=jnp.int32)[None, :]
    phase_angle = (
        sign * 2.0 * math.pi / (size_a * size_b) * (first_axis * second).astype(jnp.float32)
    )
    return (jnp.cos(phase_angle), jnp.sin(phase_angle))


def complex_mix(pattern, real_part, imag_part, table_real, table_imag):
    out_real = jnp.einsum(pattern, real_part, table_real, precision=highest) - jnp.einsum(
        pattern, imag_part, table_imag, precision=highest
    )
    out_imag = jnp.einsum(pattern, real_part, table_imag, precision=highest) + jnp.einsum(
        pattern, imag_part, table_real, precision=highest
    )
    return (out_real, out_imag)


def rotate(real_part, imag_part, cosine, sine_part):
    return (real_part * cosine - imag_part * sine_part, real_part * sine_part + imag_part * cosine)


def local_forward(real_part, imag_part):
    leading = real_part.shape[:-1]
    seq_width = real_part.shape[-1]
    size_a = seq_width // lane_width
    real_part = real_part.reshape(-1, size_a, lane_width)
    imag_part = imag_part.reshape(-1, size_a, lane_width)
    table_real, table_imag = dft_table(size_a, -1.0)
    real_part, imag_part = complex_mix("xab,ac->xcb", real_part, imag_part, table_real, table_imag)
    cosine, sine_part = cross_table(size_a, lane_width, -1.0)
    real_part, imag_part = rotate(real_part, imag_part, cosine, sine_part)
    table_real, table_imag = dft_table(lane_width, -1.0)
    real_part, imag_part = complex_mix("xcb,bd->xcd", real_part, imag_part, table_real, table_imag)
    return (real_part.reshape(leading + (seq_width,)), imag_part.reshape(leading + (seq_width,)))


def local_inverse(real_part, imag_part):
    leading = real_part.shape[:-1]
    seq_width = real_part.shape[-1]
    size_a = seq_width // lane_width
    real_part = real_part.reshape(-1, size_a, lane_width)
    imag_part = imag_part.reshape(-1, size_a, lane_width)
    table_real, table_imag = dft_table(lane_width, 1.0)
    real_part, imag_part = complex_mix("xcd,db->xcb", real_part, imag_part, table_real, table_imag)
    cosine, sine_part = cross_table(size_a, lane_width, 1.0)
    real_part, imag_part = rotate(real_part, imag_part, cosine, sine_part)
    table_real, table_imag = dft_table(size_a, 1.0)
    real_part, imag_part = complex_mix("xcb,ca->xab", real_part, imag_part, table_real, table_imag)
    return (real_part.reshape(leading + (seq_width,)), imag_part.reshape(leading + (seq_width,)))


def spectrum_index(position, devices):
    levels = devices.bit_length() - 1
    flipped = jnp.zeros((), jnp.int32)
    for section_bit in range(levels):
        flipped = flipped + (position >> section_bit & 1) * (1 << levels - 1 - section_bit)
    return flipped


def weigh_pair(current, partner, alpha_real, alpha_imag, beta_real, beta_imag):
    new_real = (
        alpha_real * current[0]
        - alpha_imag * current[1]
        + beta_real * partner[0]
        - beta_imag * partner[1]
    )
    new_imag = (
        alpha_real * current[1]
        + alpha_imag * current[0]
        + beta_real * partner[1]
        + beta_imag * partner[0]
    )
    return jnp.stack([new_real, new_imag])


def devices_forward(current):
    devices = lax.axis_size("seq")
    position = lax.axis_index("seq")
    levels = devices.bit_length() - 1
    for section_bit in range(levels - 1, -1, -1):
        half_span = 1 << section_bit
        partner = partner_2(current, "seq", section_bit)
        upper = (position >> section_bit & 1).astype(jnp.float32)
        offset = (position & half_span - 1).astype(jnp.float32)
        phase_angle = -math.pi / half_span * offset
        cosine = jnp.cos(phase_angle)
        sine_part = jnp.sin(phase_angle)
        alpha_real = 1.0 - upper - upper * cosine
        alpha_imag = -upper * sine_part
        beta_real = 1.0 - upper + upper * cosine
        beta_imag = upper * sine_part
        current = weigh_pair(current, partner, alpha_real, alpha_imag, beta_real, beta_imag)
    return current


def devices_inverse(current):
    devices = lax.axis_size("seq")
    position = lax.axis_index("seq")
    levels = devices.bit_length() - 1
    for section_bit in range(levels):
        half_span = 1 << section_bit
        partner = partner_2(current, "seq", section_bit)
        upper = (position >> section_bit & 1).astype(jnp.float32)
        offset = (position & half_span - 1).astype(jnp.float32)
        phase_angle = math.pi / half_span * offset
        cosine = jnp.cos(phase_angle)
        sine_part = jnp.sin(phase_angle)
        alpha_real = 1.0 - upper - upper * cosine
        alpha_imag = -upper * sine_part
        beta_real = upper + (1.0 - upper) * cosine
        beta_imag = (1.0 - upper) * sine_part
        current = weigh_pair(current, partner, alpha_real, alpha_imag, beta_real, beta_imag)
    return current


def step_twiddle(position, devices, seq_width, sign):
    frequency = 2 * spectrum_index(position, devices) + jnp.arange(2, dtype=jnp.int32)
    sample = jnp.arange(seq_width, dtype=jnp.int32)
    phase_angle = (
        sign
        * 2.0
        * math.pi
        / (2 * devices * seq_width)
        * (frequency[:, None] * sample[None, :]).astype(jnp.float32)
    )
    return (jnp.cos(phase_angle)[:, None, :], jnp.sin(phase_angle)[:, None, :])


def forward_spectrum(signal):
    devices = lax.axis_size("seq")
    position = lax.axis_index("seq")
    seq_width = signal.shape[1]
    phase_angle = -math.pi / devices * position.astype(jnp.float32)
    current = jnp.stack(
        [
            jnp.stack([signal, signal * jnp.cos(phase_angle)]),
            jnp.stack([jnp.zeros_like(signal), signal * jnp.sin(phase_angle)]),
        ]
    )
    current = devices_forward(current)
    cosine, sine_part = step_twiddle(position, devices, seq_width, -1.0)
    real_part, imag_part = rotate(current[0], current[1], cosine, sine_part)
    return local_forward(real_part, imag_part)


def inverse_signal(real_part, imag_part):
    devices = lax.axis_size("seq")
    position = lax.axis_index("seq")
    seq_width = real_part.shape[2]
    real_part, imag_part = local_inverse(real_part, imag_part)
    cosine, sine_part = step_twiddle(position, devices, seq_width, 1.0)
    real_part, imag_part = rotate(real_part, imag_part, cosine, sine_part)
    current = devices_inverse(jnp.stack([real_part, imag_part]))
    phase_angle = math.pi / devices * position.astype(jnp.float32)
    turned_real = current[0, 1] * jnp.cos(phase_angle) - current[1, 1] * jnp.sin(phase_angle)
    turned_imag = current[0, 1] * jnp.sin(phase_angle) + current[1, 1] * jnp.cos(phase_angle)
    norm_factor = 2.0 * devices * seq_width
    return (
        (current[0, 0] + turned_real) / norm_factor,
        (current[1, 0] + turned_imag) / norm_factor,
    )


def shards(gate_query, gate_key, gate_value, filters, upstream):
    channel_rows = gate_value.shape[0]
    seq_width = gate_value.shape[1]
    tap_scale = 1.0 / math.sqrt(lax.axis_size("seq") * seq_width)
    query_gate = gate_query.astype(jnp.float32)
    key_gate = gate_key.astype(jnp.float32)
    value_gate = gate_value.astype(jnp.float32)
    upstream_f32 = upstream.astype(jnp.float32)
    signal = key_gate * value_gate
    grad_gate = upstream_f32 * query_gate
    filter_tap = lax.all_to_all(filters, "ch", split_axis=0, concat_axis=1, tiled=True) * tap_scale
    filter_count = filter_tap.shape[0]
    group_width = channel_rows // filter_count
    real_part, imag_part = forward_spectrum(
        jnp.concatenate([signal, grad_gate, filter_tap], axis=0)
    )

    def grouped(block):
        return block.reshape(2, filter_count, group_width, seq_width)

    taps_real = real_part[:, 2 * channel_rows :][:, :, None, :]
    taps_imag = imag_part[:, 2 * channel_rows :][:, :, None, :]
    signal_real = grouped(real_part[:, :channel_rows])
    signal_imag = grouped(imag_part[:, :channel_rows])
    grad_real = grouped(real_part[:, channel_rows : 2 * channel_rows])
    grad_imag = grouped(imag_part[:, channel_rows : 2 * channel_rows])
    flat_shape = (2, channel_rows, seq_width)
    mixed_real = (signal_real * taps_real - signal_imag * taps_imag).reshape(flat_shape)
    mixed_imag = (signal_real * taps_imag + signal_imag * taps_real).reshape(flat_shape)
    back_real = (grad_real * taps_real + grad_imag * taps_imag).reshape(flat_shape)
    back_imag = (grad_imag * taps_real - grad_real * taps_imag).reshape(flat_shape)
    cross_real = jnp.sum(grad_real * signal_real + grad_imag * signal_imag, axis=2)
    cross_imag = jnp.sum(grad_imag * signal_real - grad_real * signal_imag, axis=2)
    leading_real = mixed_real - back_imag
    leading_imag = mixed_imag + back_real
    field_real, field_imag = inverse_signal(
        jnp.concatenate([leading_real, cross_real], axis=1),
        jnp.concatenate([leading_imag, cross_imag], axis=1),
    )
    grad_taps = field_real[channel_rows:] * tap_scale
    grad_filters = lax.all_to_all(grad_taps, "ch", split_axis=1, concat_axis=0, tiled=True)
    mixed_field = field_real[:channel_rows]
    grad_signal = field_imag[:channel_rows]
    mixed = (query_gate * mixed_field).astype(jnp.bfloat16)
    grad_query = (upstream_f32 * mixed_field).astype(jnp.bfloat16)
    grad_key = (grad_signal * value_gate).astype(jnp.bfloat16)
    grad_value = (grad_signal * key_gate).astype(jnp.bfloat16)
    return (mixed, grad_query, grad_key, grad_value, grad_filters)


def solution(mesh):
    in_specs = (
        P("ch", "seq"),
        P("ch", "seq"),
        P("ch", "seq"),
        P(None, ("seq", "ch")),
        P("ch", "seq"),
    )
    out_specs = (
        P("ch", "seq"),
        P("ch", "seq"),
        P("ch", "seq"),
        P("ch", "seq"),
        P(None, ("seq", "ch")),
    )
    return jax.shard_map(shards, mesh=mesh, in_specs=in_specs, out_specs=out_specs, check_vma=False)
```

profile of v0, /device:TPU:96, one launch (start us, length us, event | category | flops | bytes accessed | tf_op | source)
XLA Modules:
  0.0 550.5 jit_solution(7308109809001946172)
XLA Ops:
  2.1 4.3 all-to-all-start
  8.4 3.4 all-to-all-done
  13.5 5.1 collective-permute-start
  18.8 23.7 %collective-permute-done = f32[2,2,528,128]{3,2,1,0:T(8,128)S(1)} collective-permute-done((f32[2,2,528,128]{3,2,1,0:T(8,128)S(1)}, f32[2,2,528,128]{3,2,1,0:T(8,128)S(1)}, u32[]{:S(2)}, u32[]{:S(2)}) %collective-permute-start) | collective-permute-done | bytes 1081376 | tf_op jit(solution)/shard_map/ppermute | solution.py:15
  42.8 3.5 collective-permute-start.1
  46.5 22.9 %collective-permute-done.1 = f32[2,2,528,128]{3,2,1,0:T(8,128)S(1)} collective-permute-done((f32[2,2,528,128]{3,2,1,0:T(8,128)S(1)}, f32[2,2,528,128]{3,2,1,0:T(8,128)S(1)}, u32[]{:S(2)}, u32[]{:S(2)}) %collective-permute-start.1) | collective-permute-done | bytes 1081376 | tf_op jit(solution)/shard_map/ppermute | solution.py:15
  69.7 13.0 %collective-permute-start.2 = (f32[2,2,528,128]{3,2,1,0:T(8,128)S(1)}, f32[2,2,528,128]{3,2,1,0:T(8,128)S(1)}, u32[]{:S(2)}, u32[]{:S(2)}) collective-permute-start(f32[2,2,528,128]{3,2,1,0:T(8,128)S(1)} %pad_maximum_fusion.2), channel_id=1, source_target_pairs={{0,64},{8,72},{16,80},{24,88},{32,96},{40,104},{48,112},{56,120},{... | collective-permute-start | bytes 3244040 | tf_op jit(solution)/shard_map/ppermute | solution.py:15
  82.9 79.8 %collective-permute-done.2 = f32[2,2,528,128]{3,2,1,0:T(8,128)S(1)} collective-permute-done((f32[2,2,528,128]{3,2,1,0:T(8,128)S(1)}, f32[2,2,528,128]{3,2,1,0:T(8,128)S(1)}, u32[]{:S(2)}, u32[]{:S(2)}) %collective-permute-start.2) | collective-permute-done | bytes 1081376 | tf_op jit(solution)/shard_map/ppermute | solution.py:15
  163.1 3.5 collective-permute-start.3
  166.7 99.5 %collective-permute-done.3 = f32[2,2,528,128]{3,2,1,0:T(8,128)S(1)} collective-permute-done((f32[2,2,528,128]{3,2,1,0:T(8,128)S(1)}, f32[2,2,528,128]{3,2,1,0:T(8,128)S(1)}, u32[]{:S(2)}, u32[]{:S(2)}) %collective-permute-start.3) | collective-permute-done | bytes 1081376 | tf_op jit(solution)/shard_map/ppermute | solution.py:15
  268.7 49.7 %collective-permute-done.4 = f32[2,2,528,128]{3,2,1,0:T(8,128)S(1)} collective-permute-done((f32[2,2,528,128]{3,2,1,0:T(8,128)S(1)}, f32[2,2,528,128]{3,2,1,0:T(8,128)S(1)}, u32[]{:S(2)}, u32[]{:S(2)}) %collective-permute-start.4) | collective-permute-done | bytes 1081376 | tf_op jit(solution)/shard_map/ppermute | solution.py:15
  320.8 24.7 %collective-permute-done.5 = f32[2,2,528,128]{3,2,1,0:T(8,128)S(1)} collective-permute-done((f32[2,2,528,128]{3,2,1,0:T(8,128)S(1)}, f32[2,2,528,128]{3,2,1,0:T(8,128)S(1)}, u32[]{:S(2)}, u32[]{:S(2)}) %collective-permute-start.5) | collective-permute-done | bytes 1081376 | tf_op jit(solution)/shard_map/ppermute | solution.py:15
  354.7 12.5 %collective-permute-done.6 = f32[2,2,272,128]{3,2,1,0:T(8,128)S(1)} collective-permute-done((f32[2,2,272,128]{3,2,1,0:T(8,128)S(1)}, f32[2,2,272,128]{3,2,1,0:T(8,128)S(1)}, u32[]{:S(2)}, u32[]{:S(2)}) %collective-permute-start.6) | collective-permute-done | bytes 557088 | tf_op jit(solution)/shard_map/ppermute | solution.py:15
  367.3 4.0 collective-permute-start.7
  371.5 23.1 %collective-permute-done.7 = f32[2,2,272,128]{3,2,1,0:T(8,128)S(1)} collective-permute-done((f32[2,2,272,128]{3,2,1,0:T(8,128)S(1)}, f32[2,2,272,128]{3,2,1,0:T(8,128)S(1)}, u32[]{:S(2)}, u32[]{:S(2)}) %collective-permute-start.7) | collective-permute-done | bytes 557088 | tf_op jit(solution)/shard_map/ppermute | solution.py:15
  394.8 4.6 collective-permute-start.8
  399.5 56.8 %collective-permute-done.8 = f32[2,2,272,128]{3,2,1,0:T(8,128)S(1)} collective-permute-done((f32[2,2,272,128]{3,2,1,0:T(8,128)S(1)}, f32[2,2,272,128]{3,2,1,0:T(8,128)S(1)}, u32[]{:S(2)}, u32[]{:S(2)}) %collective-permute-start.8) | collective-permute-done | bytes 557088 | tf_op jit(solution)/shard_map/ppermute | solution.py:15
  456.5 11.0 %collective-permute-start.9 = (f32[2,2,272,128]{3,2,1,0:T(8,128)S(1)}, f32[2,2,272,128]{3,2,1,0:T(8,128)S(1)}, u32[]{:S(2)}, u32[]{:S(2)}) collective-permute-start(f32[2,2,272,128]{3,2,1,0:T(8,128)S(1)} %pad_maximum_fusion.9), channel_id=1, source_target_pairs={{0,64},{8,72},{16,80},{24,88},{32,96},{40,104},{48,112},{56,120},{... | collective-permute-start | bytes 1671176 | tf_op jit(solution)/shard_map/ppermute | solution.py:15
  467.6 37.2 %collective-permute-done.9 = f32[2,2,272,128]{3,2,1,0:T(8,128)S(1)} collective-permute-done((f32[2,2,272,128]{3,2,1,0:T(8,128)S(1)}, f32[2,2,272,128]{3,2,1,0:T(8,128)S(1)}, u32[]{:S(2)}, u32[]{:S(2)}) %collective-permute-start.9) | collective-permute-done | bytes 557088 | tf_op jit(solution)/shard_map/ppermute | solution.py:15
  505.0 3.5 collective-permute-start.10
  508.7 12.8 %collective-permute-done.10 = f32[2,2,272,128]{3,2,1,0:T(8,128)S(1)} collective-permute-done((f32[2,2,272,128]{3,2,1,0:T(8,128)S(1)}, f32[2,2,272,128]{3,2,1,0:T(8,128)S(1)}, u32[]{:S(2)}, u32[]{:S(2)}) %collective-permute-start.10) | collective-permute-done | bytes 557088 | tf_op jit(solution)/shard_map/ppermute | solution.py:15
  521.7 5.1 collective-permute-start.11
  527.1 11.7 %collective-permute-done.11 = f32[2,2,272,128]{3,2,1,0:T(8,128)S(1)} collective-permute-done((f32[2,2,272,128]{3,2,1,0:T(8,128)S(1)}, f32[2,2,272,128]{3,2,1,0:T(8,128)S(1)}, u32[]{:S(2)}, u32[]{:S(2)}) %collective-permute-start.11) | collective-permute-done | bytes 557088 | tf_op jit(solution)/shard_map/ppermute | solution.py:15
  545.2 3.9 all-to-all-done.1
  (81 shorter events, 28.2 us)
Async XLA Ops:
  2.1 9.6 %all-to-all-start = ((f32[8,1,256]{2,1,0:T(1,128)}), f32[8,1,256]{2,1,0:T(1,128)S(1)}, u32[]{:S(2)}, u32[]{:S(2)}) async-start(f32[8,1,256]{2,1,0:T(1,128)} %reshape.515), calls=%async_computation | async-start | bytes 16384 | tf_op jit(solution)/shard_map/all_to_all | solution.py:200
  13.5 29.0 %collective-permute-start = (f32[2,2,528,128]{3,2,1,0:T(8,128)S(1)}, f32[2,2,528,128]{3,2,1,0:T(8,128)S(1)}, u32[]{:S(2)}, u32[]{:S(2)}) collective-permute-start(f32[2,2,528,128]{3,2,1,0:T(8,128)S(1)} %pad_maximum_fusion), channel_id=1, source_target_pairs={{0,256},{8,264},{16,272},{24,280},{32,288},{40,296},{48,304},{56,3... | collective-permute-start | bytes 3244040 | tf_op jit(solution)/shard_map/ppermute | solution.py:15
  42.8 26.6 %collective-permute-start.1 = (f32[2,2,528,128]{3,2,1,0:T(8,128)S(1)}, f32[2,2,528,128]{3,2,1,0:T(8,128)S(1)}, u32[]{:S(2)}, u32[]{:S(2)}) collective-permute-start(f32[2,2,528,128]{3,2,1,0:T(8,128)S(1)} %pad_maximum_fusion.1), channel_id=1, source_target_pairs={{0,128},{8,136},{16,144},{24,152},{32,160},{40,168},{48,176},{56,1... | collective-permute-start | bytes 3244040 | tf_op jit(solution)/shard_map/ppermute | solution.py:15
  69.7 93.0 %collective-permute-start.2 = (f32[2,2,528,128]{3,2,1,0:T(8,128)S(1)}, f32[2,2,528,128]{3,2,1,0:T(8,128)S(1)}, u32[]{:S(2)}, u32[]{:S(2)}) collective-permute-start(f32[2,2,528,128]{3,2,1,0:T(8,128)S(1)} %pad_maximum_fusion.2), channel_id=1, source_target_pairs={{0,64},{8,72},{16,80},{24,88},{32,96},{40,104},{48,112},{56,120},{... | collective-permute-start | bytes 3244040 | tf_op jit(solution)/shard_map/ppermute | solution.py:15
  163.1 103.2 %collective-permute-start.3 = (f32[2,2,528,128]{3,2,1,0:T(8,128)S(1)}, f32[2,2,528,128]{3,2,1,0:T(8,128)S(1)}, u32[]{:S(2)}, u32[]{:S(2)}) collective-permute-start(f32[2,2,528,128]{3,2,1,0:T(8,128)S(1)} %pad_maximum_fusion.3), channel_id=1, source_target_pairs={{0,32},{8,40},{16,48},{24,56},{32,0},{40,8},{48,16},{56,24},{64,96... | collective-permute-start | bytes 3244040 | tf_op jit(solution)/shard_map/ppermute | solution.py:15
  266.6 51.8 %collective-permute-start.4 = (f32[2,2,528,128]{3,2,1,0:T(8,128)S(1)}, f32[2,2,528,128]{3,2,1,0:T(8,128)S(1)}, u32[]{:S(2)}, u32[]{:S(2)}) collective-permute-start(f32[2,2,528,128]{3,2,1,0:T(8,128)S(1)} %pad_maximum_fusion.4), channel_id=1, source_target_pairs={{0,16},{8,24},{16,0},{24,8},{32,48},{40,56},{48,32},{56,40},{64,80... | collective-permute-start | bytes 3244040 | tf_op jit(solution)/shard_map/ppermute | solution.py:15
  318.7 26.8 %collective-permute-start.5 = (f32[2,2,528,128]{3,2,1,0:T(8,128)S(1)}, f32[2,2,528,128]{3,2,1,0:T(8,128)S(1)}, u32[]{:S(2)}, u32[]{:S(2)}) collective-permute-start(f32[2,2,528,128]{3,2,1,0:T(8,128)S(1)} %pad_maximum_fusion.5), channel_id=1, source_target_pairs={{0,8},{8,0},{16,24},{24,16},{32,40},{40,32},{48,56},{56,48},{64,72... | collective-permute-start | bytes 3244040 | tf_op jit(solution)/shard_map/ppermute | solution.py:15
  352.4 14.7 %collective-permute-start.6 = (f32[2,2,272,128]{3,2,1,0:T(8,128)S(1)}, f32[2,2,272,128]{3,2,1,0:T(8,128)S(1)}, u32[]{:S(2)}, u32[]{:S(2)}) collective-permute-start(f32[2,2,272,128]{3,2,1,0:T(8,128)S(1)} %pad_maximum_fusion.6), channel_id=1, source_target_pairs={{0,8},{8,0},{16,24},{24,16},{32,40},{40,32},{48,56},{56,48},{64,72... | collective-permute-start | bytes 1671176 | tf_op jit(solution)/shard_map/ppermute | solution.py:15
  367.3 27.3 %collective-permute-start.7 = (f32[2,2,272,128]{3,2,1,0:T(8,128)S(1)}, f32[2,2,272,128]{3,2,1,0:T(8,128)S(1)}, u32[]{:S(2)}, u32[]{:S(2)}) collective-permute-start(f32[2,2,272,128]{3,2,1,0:T(8,128)S(1)} %pad_maximum_fusion.7), channel_id=1, source_target_pairs={{0,16},{8,24},{16,0},{24,8},{32,48},{40,56},{48,32},{56,40},{64,80... | collective-permute-start | bytes 1671176 | tf_op jit(solution)/shard_map/ppermute | solution.py:15
  394.8 61.6 %collective-permute-start.8 = (f32[2,2,272,128]{3,2,1,0:T(8,128)S(1)}, f32[2,2,272,128]{3,2,1,0:T(8,128)S(1)}, u32[]{:S(2)}, u32[]{:S(2)}) collective-permute-start(f32[2,2,272,128]{3,2,1,0:T(8,128)S(1)} %pad_maximum_fusion.8), channel_id=1, source_target_pairs={{0,32},{8,40},{16,48},{24,56},{32,0},{40,8},{48,16},{56,24},{64,96... | collective-permute-start | bytes 1671176 | tf_op jit(solution)/shard_map/ppermute | solution.py:15
  456.5 48.3 %collective-permute-start.9 = (f32[2,2,272,128]{3,2,1,0:T(8,128)S(1)}, f32[2,2,272,128]{3,2,1,0:T(8,128)S(1)}, u32[]{:S(2)}, u32[]{:S(2)}) collective-permute-start(f32[2,2,272,128]{3,2,1,0:T(8,128)S(1)} %pad_maximum_fusion.9), channel_id=1, source_target_pairs={{0,64},{8,72},{16,80},{24,88},{32,96},{40,104},{48,112},{56,120},{... | collective-permute-start | bytes 1671176 | tf_op jit(solution)/shard_map/ppermute | solution.py:15
  505.0 16.4 %collective-permute-start.10 = (f32[2,2,272,128]{3,2,1,0:T(8,128)S(1)}, f32[2,2,272,128]{3,2,1,0:T(8,128)S(1)}, u32[]{:S(2)}, u32[]{:S(2)}) collective-permute-start(f32[2,2,272,128]{3,2,1,0:T(8,128)S(1)} %pad_maximum_fusion.10), channel_id=1, source_target_pairs={{0,128},{8,136},{16,144},{24,152},{32,160},{40,168},{48,176},{56,1... | collective-permute-start | bytes 1671176 | tf_op jit(solution)/shard_map/ppermute | solution.py:15
  521.7 17.1 %collective-permute-start.11 = (f32[2,2,272,128]{3,2,1,0:T(8,128)S(1)}, f32[2,2,272,128]{3,2,1,0:T(8,128)S(1)}, u32[]{:S(2)}, u32[]{:S(2)}) collective-permute-start(f32[2,2,272,128]{3,2,1,0:T(8,128)S(1)} %pad_maximum_fusion.11), channel_id=1, source_target_pairs={{0,256},{8,264},{16,272},{24,280},{32,288},{40,296},{48,304},{56,3... | collective-permute-start | bytes 1671176 | tf_op jit(solution)/shard_map/ppermute | solution.py:15
  527.1 11.9 %copy-start.1 = (bf16[256,128]{1,0:T(8,128)(2,1)S(1)}, bf16[256,128]{1,0:T(8,128)(2,1)}, u32[]{:S(2)}) copy-start(bf16[256,128]{1,0:T(8,128)(2,1)} %param.9) | copy-start | bytes 196612
  527.1 11.9 %copy-start.2 = (bf16[256,128]{1,0:T(8,128)(2,1)S(1)}, bf16[256,128]{1,0:T(8,128)(2,1)}, u32[]{:S(2)}) copy-start(bf16[256,128]{1,0:T(8,128)(2,1)} %param.5) | copy-start | bytes 196612
  538.9 4.9 copy-start
  538.9 5.6 %copy-start.3 = (bf16[256,128]{1,0:T(8,128)(2,1)S(1)}, bf16[256,128]{1,0:T(8,128)(2,1)}, u32[]{:S(2)}) copy-start(bf16[256,128]{1,0:T(8,128)(2,1)} %param.7) | copy-start | bytes 196612
  540.5 8.6 %all-to-all-start.1 = ((f32[8,1,256]{2,1,0:T(1,128)}), f32[8,1,256]{2,1,0:T(1,128)S(1)}, u32[]{:S(2)}, u32[]{:S(2)}) async-start(f32[8,1,256]{2,1,0:T(1,128)} %reshape.517), calls=%async_computation.1 | async-start | bytes 16384 | tf_op jit(solution)/shard_map/all_to_all | solution.py:230
where the time goes:
time: 551 us
  waiting for transfers between devices  462 us (84%)
  starting transfers between devices  66.9 us (12%)
  other arithmetic  8.97 us (2%)
  matrix products  5.86 us (1%)
    ppermute x12, waiting for transfers between devices, partner_2(): return lax.ppermute(value, axis, pairs)  454 us
    ppermute x12, starting transfers between devices, partner_2(): return lax.ppermute(value, axis, pairs)  59.2 us
  transfers between devices with their start and end apart: 14, of which 14 were waited for; matrix products, arithmetic and copies ran while one was open for 1% of the time, Pallas kernels for 0%

commit v1 on v0

v1 whole, which is shorter than its diff:
```python
import functools
import math

import jax
import jax.numpy as jnp
import ml_dtypes
import numpy as np
from jax import lax
from jax.experimental import pallas as pl
from jax.experimental.pallas import tpu as pltpu
from jax.sharding import PartitionSpec as P

f32 = jnp.float32
bf16 = jnp.bfloat16
vmem = pl.BlockSpec(memory_space=pltpu.VMEM)


def halves(table):
    high = table.astype(ml_dtypes.bfloat16)
    low = (table - high.astype(np.float64)).astype(ml_dtypes.bfloat16)
    return high, low


def make_tables(parts, width):
    total = parts * width
    k1 = np.arange(parts) + 0.25
    p = np.arange(parts)
    b = np.arange(width)
    outer = 2.0 * np.pi / parts * (k1[:, None] * p[None, :])
    first = np.concatenate([np.cos(outer), -np.sin(outer)], axis=0)
    last = np.concatenate([np.cos(outer.T), -np.sin(outer.T)], axis=1) / total
    turn = 2.0 * np.pi / total * (k1[:, None] * b[None, :])
    twiddle = np.concatenate([np.cos(turn), -np.sin(turn)], axis=1).astype(np.float32)
    inner = 2.0 * np.pi / width * (b[:, None] * b[None, :] % width)
    cosine, sine = np.cos(inner), np.sin(inner)
    forward = np.block([[cosine, -sine], [sine, cosine]])
    inverse = np.block([[cosine, sine], [-sine, cosine]])
    first_high, first_low = halves(first)
    last_high, last_low = halves(last)
    return dict(
        first=np.concatenate([first_high, first_high, first_low], axis=1),
        last=np.concatenate([last_high, last_high, last_low], axis=1),
        twiddle=twiddle,
        forward=np.stack(halves(forward)),
        inverse=np.stack(halves(inverse)),
    )


def split(value):
    high = value.astype(bf16)
    return high, (value - high.astype(f32)).astype(bf16)


def dot(left, right):
    return jnp.dot(left, right, preferred_element_type=f32)


def stacked_dot(table, value):
    high, low = split(value)
    return dot(table, jnp.concatenate([high, low, high], axis=0))


def table_dot(value, table_ref):
    high, low = split(value)
    return dot(high, table_ref[0]) + (dot(low, table_ref[0]) + dot(high, table_ref[1]))


def to_spectrum(rows, first_ref, twiddle_ref, forward_ref):
    parts, width = rows[0].shape
    stage = stacked_dot(first_ref[...], jnp.concatenate(rows, axis=1))
    cosine, sine = twiddle_ref[:, :width], twiddle_ref[:, width:]
    turned = []
    for r in range(len(rows)):
        real = stage[:parts, r * width : (r + 1) * width]
        imag = stage[parts:, r * width : (r + 1) * width]
        turned.append(
            jnp.concatenate([real * cosine - imag * sine, real * sine + imag * cosine], axis=1)
        )
    return table_dot(jnp.concatenate(turned, axis=0), forward_ref)


def from_spectrum(spectrum, last_ref, twiddle_ref, inverse_ref):
    parts = last_ref.shape[0]
    width = spectrum.shape[1] // 2
    stage = table_dot(spectrum, inverse_ref)
    cosine, sine = twiddle_ref[:, :width], twiddle_ref[:, width:]
    turned = []
    for r in range(stage.shape[0] // parts):
        real = stage[r * parts : (r + 1) * parts, :width]
        imag = stage[r * parts : (r + 1) * parts, width:]
        turned.append(
            jnp.concatenate([real * cosine + imag * sine, imag * cosine - real * sine], axis=0)
        )
    return stacked_dot(last_ref[...], jnp.concatenate(turned, axis=1))


def times(a, b):
    w = a.shape[1] // 2
    ar, ai, br, bi = a[:, :w], a[:, w:], b[:, :w], b[:, w:]
    return jnp.concatenate([ar * br - ai * bi, ar * bi + ai * br], axis=1)


def times_conj(a, b):
    w = a.shape[1] // 2
    ar, ai, br, bi = a[:, :w], a[:, w:], b[:, :w], b[:, w:]
    return jnp.concatenate([ar * br + ai * bi, ai * br - ar * bi], axis=1)


def lane_blocks(pieces):
    count = len(pieces)
    block = pieces[0].shape[1] // count
    lane = lax.broadcasted_iota(jnp.int32, pieces[0].shape, 1) // block
    out = []
    for c in range(count):
        total = pieces[0] if c == 0 else pltpu.roll(pieces[0], (-c) % count * block, 1)
        for a in range(1, count):
            shift = (a - c) % count * block
            moved = pieces[a] if shift == 0 else pltpu.roll(pieces[a], shift, 1)
            total = jnp.where(lane == a, moved, total)
        out.append(total)
    return out


def gates_kernel(sizes, query_ref, key_ref, value_ref, filters_ref, upstream_ref, out_ref, rows_ref):
    parts, channels, own, groups = sizes
    rows = 2 * own + 1
    filter_count = filters_ref.shape[0] // groups
    share = parts // filter_count
    rows_ref[0] = key_ref[...].astype(f32) * value_ref[...].astype(f32)
    rows_ref[1] = upstream_ref[...].astype(f32) * query_ref[...].astype(f32)
    for which in range(2):
        for j in range(own):
            out_ref[pl.ds(which * own + j, parts, stride=rows), :] = rows_ref[
                which, pl.ds(j, parts, stride=own), :
            ]
    side = jnp.concatenate(
        [filters_ref[g * filter_count : (g + 1) * filter_count, :] for g in range(groups)], axis=1
    )
    for i in range(share):
        out_ref[pl.ds(2 * own + rows * i, filter_count, stride=rows * share), :] = side


def spectra_kernel(
    sizes, x_ref, first_ref, twiddle_ref, forward_ref, inverse_ref, last_ref, spec_ref, out_ref
):
    parts, channels, own, groups = sizes
    rows = 2 * own + 1
    blocks = [x_ref[pl.ds(r, parts, stride=rows), :] for r in range(rows)]
    spectrum = to_spectrum(blocks[: 2 * own], first_ref, twiddle_ref, forward_ref)
    spec_ref[...] = spectrum
    cross = None
    for j in range(own):
        term = times_conj(
            spectrum[(own + j) * parts : (own + j + 1) * parts],
            spectrum[j * parts : (j + 1) * parts],
        )
        cross = term if cross is None else cross + term
    grad_taps = from_spectrum(cross, last_ref, twiddle_ref, inverse_ref)
    for which, block in enumerate((blocks[2 * own], grad_taps)):
        count = parts // groups
        pieces = lane_blocks([block[a * count : (a + 1) * count] for a in range(groups)])
        for g in range(groups):
            out_ref[g, which * count : (which + 1) * count, :] = pieces[g]


def fields_kernel(
    sizes, tap_scale, spec_ref, side_ref, first_ref, twiddle_ref, forward_ref, inverse_ref, last_ref, out_ref
):
    parts, channels, own, groups = sizes
    rows = 2 * own + 1
    count = parts // groups
    taps, grad_taps = (
        jnp.concatenate(
            lane_blocks([side_ref[g, which * count : (which + 1) * count, :] for g in range(groups)]),
            axis=0,
        )
        for which in range(2)
    )
    out_ref[pl.ds(2 * own, parts, stride=rows), :] = grad_taps * tap_scale
    taps = to_spectrum([taps * tap_scale], first_ref, twiddle_ref, forward_ref)
    products = []
    for j in range(own):
        products.append(times(spec_ref[j * parts : (j + 1) * parts, :], taps))
    for j in range(own, 2 * own):
        products.append(times_conj(spec_ref[j * parts : (j + 1) * parts, :], taps))
    fields = from_spectrum(jnp.concatenate(products, axis=0), last_ref, twiddle_ref, inverse_ref)
    width = fields.shape[1] // (2 * own)
    for r in range(2 * own):
        out_ref[pl.ds(r, parts, stride=rows), :] = fields[:, r * width : (r + 1) * width]


def outputs_kernel(
    sizes,
    y_ref,
    query_ref,
    key_ref,
    value_ref,
    upstream_ref,
    mixed_ref,
    grad_query_ref,
    grad_key_ref,
    grad_value_ref,
    grad_filters_ref,
    rows_ref,
):
    parts, channels, own, groups = sizes
    rows = 2 * own + 1
    filter_count = grad_filters_ref.shape[0] // groups
    share = parts // filter_count
    for which in range(2):
        for j in range(own):
            rows_ref[which, pl.ds(j, parts, stride=own), :] = y_ref[
                pl.ds(which * own + j, parts, stride=rows), :
            ]
    mixed_field = rows_ref[0]
    grad_signal = rows_ref[1]
    mixed_ref[...] = (query_ref[...].astype(f32) * mixed_field).astype(bf16)
    grad_query_ref[...] = (upstream_ref[...].astype(f32) * mixed_field).astype(bf16)
    grad_key_ref[...] = (grad_signal * value_ref[...].astype(f32)).astype(bf16)
    grad_value_ref[...] = (grad_signal * key_ref[...].astype(f32)).astype(bf16)
    side = None
    for i in range(share):
        term = y_ref[pl.ds(2 * own + rows * i, filter_count, stride=rows * share), :]
        side = term if side is None else side + term
    block = side.shape[1] // groups
    for g in range(groups):
        grad_filters_ref[g * filter_count : (g + 1) * filter_count, :] = side[
            :, g * block : (g + 1) * block
        ]


def call(kernel, out_shape, scratch=()):
    return pl.pallas_call(
        kernel,
        out_shape=out_shape,
        out_specs=jax.tree.map(lambda _: vmem, out_shape),
        scratch_shapes=scratch,
        compiler_params=pltpu.CompilerParams(vmem_limit_bytes=32 * 1024 * 1024),
    )


def shards(gate_query, gate_key, gate_value, filters, upstream):
    channels, width = gate_value.shape
    parts = lax.axis_size("seq")
    groups = lax.axis_size("ch")
    own = channels // parts
    rows = 2 * own + 1
    sizes = (parts, channels, own, groups)
    tap_scale = 1.0 / math.sqrt(parts * width)
    tables = make_tables(parts, width)
    first, twiddle, forward, inverse, last = (
        jnp.asarray(tables[name]) for name in ("first", "twiddle", "forward", "inverse", "last")
    )

    def exchange(block):
        block = block.reshape(parts, rows, 1, width)
        block = lax.all_to_all(block, "seq", split_axis=0, concat_axis=0, tiled=True)
        return block.reshape(parts * rows, width)

    shape = jax.ShapeDtypeStruct
    packed = call(
        functools.partial(gates_kernel, sizes),
        shape((parts * rows, width), f32),
        [pltpu.VMEM((2, channels, width), f32)],
    )(gate_query, gate_key, gate_value, filters, upstream)
    packed = exchange(packed)
    spectra, side = call(
        functools.partial(spectra_kernel, sizes),
        (
            shape((2 * own * parts, 2 * width), f32),
            shape((groups, 2 * parts // groups, width), f32),
        ),
    )(packed, first, twiddle, forward, inverse, last)
    side = lax.all_to_all(side, "ch", split_axis=0, concat_axis=0, tiled=True)
    packed = call(functools.partial(fields_kernel, sizes, tap_scale), shape((parts * rows, width), f32))(
        spectra, side, first, twiddle, forward, inverse, last
    )
    packed = exchange(packed)
    gates = shape((channels, width), bf16)
    return call(
        functools.partial(outputs_kernel, sizes),
        (gates, gates, gates, gates, shape(filters.shape, f32)),
        [pltpu.VMEM((2, channels, width), f32)],
    )(packed, gate_query, gate_key, gate_value, upstream)


def solution(mesh):
    in_specs = (
        P("ch", "seq"),
        P("ch", "seq"),
        P("ch", "seq"),
        P(None, ("seq", "ch")),
        P("ch", "seq"),
    )
    out_specs = (
        P("ch", "seq"),
        P("ch", "seq"),
        P("ch", "seq"),
        P("ch", "seq"),
        P(None, ("seq", "ch")),
    )
    return jax.shard_map(shards, mesh=mesh, in_specs=in_specs, out_specs=out_specs, check_vma=False)
```

time: 551 us -> 87.5 us (0.16)
  the two profiles are of different devices: /device:TPU:96 before, /device:TPU:24 now
where the time goes in v1:
time: 87.5 us; the launch traced here: 87.1 us
  blocking collectives  79.2 us (91%)
  local copies, waits for them, and re-layouts  4.06 us (5%)
  Pallas kernels  3.05 us (3%)
    all_to_all x2, blocking collectives, exchange(): lax.all_to_all(block, 'seq', split_axis=0, concat_axis=0, tiled=True)  69.5 us
    all_to_all x1, blocking collectives, shards(): side = lax.all_to_all(side, 'ch', split_axis=0, concat_axis=0, tiled=True)  9.72 us
    unnamed x25, local copies, waits for them, and re-layouts  3.39 us

profile of v1, /device:TPU:24, one launch (start us, length us, event | category | flops | bytes accessed | tf_op | source)
XLA Modules:
  0.0 87.1 jit_solution(8853346411566770631)
XLA Ops:
  0.6 0.0 copy-start.2
  0.6 0.8 copy.19.filters_ref
  1.5 0.0 copy-done.2
  1.5 0.0 copy-start.3
  1.5 0.8 copy-done.3
  2.3 0.8 copy-done.5
  3.2 0.8 copy-done.7
  4.0 0.1 shard_map.137
  4.1 0.0 copy-start
  4.1 0.0 copy-start.1
  4.1 0.0 copy-start.9
  4.1 40.9 %all_to_all.15 = f32[64,9,1,128]{3,2,1,0:T(1,128)S(1)} all-to-all(f32[64,9,1,128]{3,2,1,0:T(1,128)S(1)} %bitcast.5), channel_id=1, replica_groups=mesh['seq'=64,'ch'=8] {'seq'}, dimensions={0} | all-to-all | bytes 589824 | tf_op jit(solution)/shard_map/all_to_all | solution.py:257
  45.0 0.0 copy-done.10
  45.0 0.0 copy-done.11
  45.0 0.0 copy-done
  45.0 1.1 %shard_map.138 = (f32[512,256]{1,0:T(8,128)S(1)}, f32[8,16,128]{2,1,0:T(8,128)S(1)}) custom-call(f32[576,128]{1,0:T(8,128)S(1)} %bitcast.7, bf16[128,192]{1,0:T(8,128)(2,1)S(1)} %copy-done.10, f32[64,256]{1,0:T(8,128)S(1)} %copy-done.9, bf16[2,256,256]{2,1,0:T(8,128)(2,1)S(1)} %copy-done.1, bf16[2,256,256]{2,1,0:T(8,128)(2,1)S(1)} %copy-done, ...), custom_call_target="tpu_custom_call" | custom-call | tf_op jit(solution)/shard_map/pallas_call | solution.py:267
  46.1 9.7 %all_to_all.16.side_ref = f32[8,16,128]{2,1,0:T(8,128)S(1)} all-to-all(f32[8,16,128]{2,1,0:T(8,128)S(1)} %get-tuple-element.8), channel_id=1, replica_groups=mesh['seq'=64,'ch'=8] {'ch'}, dimensions={0} | all-to-all | bytes 131072 | tf_op jit(solution)/shard_map/all_to_all | solution.py:274
  55.8 1.2 %shard_map.139 = f32[576,128]{1,0:T(8,128)S(1)} custom-call(f32[512,256]{1,0:T(8,128)S(1)} %get-tuple-element.7.spec_ref, f32[8,16,128]{2,1,0:T(8,128)S(1)} %all_to_all.16.side_ref, bf16[128,192]{1,0:T(8,128)(2,1)S(1)} %copy-done.10, f32[64,256]{1,0:T(8,128)S(1)} %copy-done.9, bf16[2,256,256]{2,1,0:T(8,128)(2,1)S(1)} %copy-done.1, ...), custom_call_target="tpu_custom_call" | custom-call | tf_op jit(solution)/shard_map/pallas_call | solution.py:275
  57.0 0.0 copy-start.4
  57.0 0.0 copy-start.6
  57.0 0.0 copy-start.8
  57.0 28.6 %all_to_all.17 = f32[64,9,1,128]{3,2,1,0:T(1,128)S(1)} all-to-all(f32[64,9,1,128]{3,2,1,0:T(1,128)S(1)} %bitcast.6), channel_id=1, replica_groups=mesh['seq'=64,'ch'=8] {'seq'}, dimensions={0} | all-to-all | bytes 589824 | tf_op jit(solution)/shard_map/all_to_all | solution.py:257
  85.7 0.7 shard_map.140
  86.4 0.7 copy.22
  (9 shorter events, 0.0 us)
Async XLA Ops:
  0.6 0.8 copy-start.2
  1.5 0.8 copy-start.3
  2.3 0.8 copy-start.5
  3.2 0.8 copy-start.7
  4.0 41.0 %copy-start.10 = (bf16[128,192]{1,0:T(8,128)(2,1)S(1)}, bf16[128,192]{1,0:T(8,128)(2,1)}, u32[]{:S(2)}) copy-start(bf16[128,192]{1,0:T(8,128)(2,1)} %constant.10.clone.first_ref) | copy-start | bytes 147460
  4.0 41.0 %copy-start.11 = (bf16[64,384]{1,0:T(8,128)(2,1)S(1)}, bf16[64,384]{1,0:T(8,128)(2,1)}, u32[]{:S(2)}) copy-start(bf16[64,384]{1,0:T(8,128)(2,1)} %constant.14.clone.last_ref) | copy-start | bytes 147460
  4.1 40.9 %copy-start = (bf16[2,256,256]{2,1,0:T(8,128)(2,1)S(1)}, bf16[2,256,256]{2,1,0:T(8,128)(2,1)}, u32[]{:S(2)}) copy-start(bf16[2,256,256]{2,1,0:T(8,128)(2,1)} %constant.13.clone.inverse_ref) | copy-start | bytes 786436
  4.1 40.9 %copy-start.1 = (bf16[2,256,256]{2,1,0:T(8,128)(2,1)S(1)}, bf16[2,256,256]{2,1,0:T(8,128)(2,1)}, u32[]{:S(2)}) copy-start(bf16[2,256,256]{2,1,0:T(8,128)(2,1)} %constant.12.clone.forward_ref) | copy-start | bytes 786436
  4.1 40.9 %copy-start.9 = (f32[64,256]{1,0:T(8,128)S(1)}, f32[64,256]{1,0:T(8,128)}, u32[]{:S(2)}) copy-start(f32[64,256]{1,0:T(8,128)} %constant.11.clone.twiddle_ref) | copy-start | bytes 196612
  57.0 28.6 %copy-start.4 = (bf16[256,128]{1,0:T(8,128)(2,1)S(1)}, bf16[256,128]{1,0:T(8,128)(2,1)}, u32[]{:S(2)}) copy-start(bf16[256,128]{1,0:T(8,128)(2,1)} %key_ref.3) | copy-start | bytes 196612
  57.0 28.6 %copy-start.6 = (bf16[256,128]{1,0:T(8,128)(2,1)S(1)}, bf16[256,128]{1,0:T(8,128)(2,1)}, u32[]{:S(2)}) copy-start(bf16[256,128]{1,0:T(8,128)(2,1)} %value_ref.3) | copy-start | bytes 196612
  57.0 28.6 %copy-start.8 = (bf16[256,128]{1,0:T(8,128)(2,1)S(1)}, bf16[256,128]{1,0:T(8,128)(2,1)}, u32[]{:S(2)}) copy-start(bf16[256,128]{1,0:T(8,128)(2,1)} %upstream_ref.3) | copy-start | bytes 196612

commit v2 on v1

--- a/solution.py
+++ b/solution.py
@@ -121,23 +121,43 @@
     return out
 
 
-def gates_kernel(sizes, query_ref, key_ref, value_ref, filters_ref, upstream_ref, out_ref, rows_ref):
+def gates_kernel(
+    sizes,
+    query_hbm,
+    key_hbm,
+    value_hbm,
+    upstream_hbm,
+    filters_hbm,
+    out_ref,
+    gates_ref,
+    filters_ref,
+    rows_ref,
+    sems,
+):
     parts, channels, own, groups = sizes
     rows = 2 * own + 1
-    filter_count = filters_ref.shape[0] // groups
+    filter_count = filters_ref.shape[1] // groups
     share = parts // filter_count
-    rows_ref[0] = key_ref[...].astype(f32) * value_ref[...].astype(f32)
-    rows_ref[1] = upstream_ref[...].astype(f32) * query_ref[...].astype(f32)
+    loads = [pltpu.make_async_copy(filters_hbm, filters_ref, sems.at[4])]
+    for i, source in enumerate((key_hbm, value_hbm, upstream_hbm, query_hbm)):
+        loads.append(pltpu.make_async_copy(source, gates_ref.at[i], sems.at[i]))
+    for load in loads:
+        load.start()
+    loads[0].wait()
+    taps = filters_ref[...].T
+    side = jnp.concatenate(
+        [taps[g * filter_count : (g + 1) * filter_count, :] for g in range(groups)], axis=1
+    )
+    for i in range(share):
+        out_ref[pl.ds(2 * own + rows * i, filter_count, stride=rows * share), :] = side
     for which in range(2):
+        loads[1 + 2 * which].wait()
+        loads[2 + 2 * which].wait()
+        rows_ref[which] = gates_ref[2 * which].astype(f32) * gates_ref[2 * which + 1].astype(f32)
         for j in range(own):
             out_ref[pl.ds(which * own + j, parts, stride=rows), :] = rows_ref[
                 which, pl.ds(j, parts, stride=own), :
             ]
-    side = jnp.concatenate(
-        [filters_ref[g * filter_count : (g + 1) * filter_count, :] for g in range(groups)], axis=1
-    )
-    for i in range(share):
-        out_ref[pl.ds(2 * own + rows * i, filter_count, stride=rows * share), :] = side
 
 
 def spectra_kernel(
@@ -205,7 +225,7 @@
 ):
     parts, channels, own, groups = sizes
     rows = 2 * own + 1
-    filter_count = grad_filters_ref.shape[0] // groups
+    filter_count = grad_filters_ref.shape[1] // groups
     share = parts // filter_count
     for which in range(2):
         for j in range(own):
@@ -223,19 +243,19 @@
         term = y_ref[pl.ds(2 * own + rows * i, filter_count, stride=rows * share), :]
         side = term if side is None else side + term
     block = side.shape[1] // groups
-    for g in range(groups):
-        grad_filters_ref[g * filter_count : (g + 1) * filter_count, :] = side[
-            :, g * block : (g + 1) * block
-        ]
-
-
-def call(kernel, out_shape, scratch=()):
+    grad_filters_ref[...] = jnp.concatenate(
+        [side[:, g * block : (g + 1) * block] for g in range(groups)], axis=0
+    ).T
+
+
+def call(kernel, out_shape, scratch=(), grant=32, **specs):
     return pl.pallas_call(
         kernel,
         out_shape=out_shape,
         out_specs=jax.tree.map(lambda _: vmem, out_shape),
         scratch_shapes=scratch,
-        compiler_params=pltpu.CompilerParams(vmem_limit_bytes=32 * 1024 * 1024),
+        **specs,
+        compiler_params=pltpu.CompilerParams(vmem_limit_bytes=grant * 1024 * 1024),
     )
 
 
@@ -261,8 +281,15 @@
     packed = call(
         functools.partial(gates_kernel, sizes),
         shape((parts * rows, width), f32),
-        [pltpu.VMEM((2, channels, width), f32)],
-    )(gate_query, gate_key, gate_value, filters, upstream)
+        [
+            pltpu.VMEM((4, channels, width), bf16),
+            pltpu.VMEM(filters.shape[::-1], f32),
+            pltpu.VMEM((2, channels, width), f32),
+            pltpu.SemaphoreType.DMA((5,)),
+        ],
+        grant=62,
+        in_specs=[pl.BlockSpec(memory_space=pl.ANY)] * 5,
+    )(gate_query, gate_key, gate_value, upstream, filters.T)
     packed = exchange(packed)
     spectra, side = call(
         functools.partial(spectra_kernel, sizes),
@@ -277,11 +304,12 @@
     )
     packed = exchange(packed)
     gates = shape((channels, width), bf16)
-    return call(
+    *grads, grad_filters = call(
         functools.partial(outputs_kernel, sizes),
-        (gates, gates, gates, gates, shape(filters.shape, f32)),
+        (gates, gates, gates, gates, shape(filters.shape[::-1], f32)),
         [pltpu.VMEM((2, channels, width), f32)],
     )(packed, gate_query, gate_key, gate_value, upstream)
+    return (*grads, grad_filters.T)
 
 
 def solution(mesh):

time: 87.5 us -> 85.4 us (0.976)
  local copies, waits for them, and re-layouts: 4.06 us -> 0.06 us
  Pallas kernels: 3.05 us -> 4.79 us
    unnamed x25 -> x18, local copies, waits for them, and re-layouts: 3.39 us -> 0.06 us
    pallas_call x1, Pallas kernels: 0.08 us -> 1.77 us  [shards(): call(functools.partial(gates_kernel, sizes), shape((parts * rows, width),...]
where the time goes in v2:
time: 85.4 us; the launch traced here: 85 us
  blocking collectives  79.4 us (93%)
  Pallas kernels  4.79 us (6%)
    all_to_all x2, blocking collectives, exchange(): lax.all_to_all(block, 'seq', split_axis=0, concat_axis=0, tiled=True)  69.7 us
    all_to_all x1, blocking collectives, shards(): side = lax.all_to_all(side, 'ch', split_axis=0, concat_axis=0, tiled=True)  9.72 us
    pallas_call x1, Pallas kernels, shards(): call(functools.partial(gates_kernel, sizes), shape((parts * rows, width),...  1.77 us

profile of v2, /device:TPU:24, one launch (start us, length us, event | category | flops | bytes accessed | tf_op | source)
XLA Modules:
  0.0 85.0 jit_solution(6748322639821881898)
XLA Ops:
  0.6 0.0 copy-start.7
  0.6 0.0 copy-start.8
  0.7 1.8 %shard_map.137 = f32[576,128]{1,0:T(8,128)} custom-call(bf16[256,128]{1,0:T(8,128)(2,1)} %query_ref.1, bf16[256,128]{1,0:T(8,128)(2,1)} %key_ref.1, bf16[256,128]{1,0:T(8,128)(2,1)} %value_ref.1, bf16[256,128]{1,0:T(8,128)(2,1)} %upstream_ref.1, f32[16,128]{1,0:T(8,128)} %bitcast.10), custom_call_target="tpu_custom_call" | custom-call | tf_op jit(solution)/shard_map/pallas_call | solution.py:281
  2.4 0.0 copy-start
  2.4 0.0 copy-start.1
  2.5 0.0 copy-start.6
  2.5 41.1 %all_to_all.15 = f32[64,9,1,128]{3,2,1,0:T(1,128)S(1)} all-to-all(f32[64,9,1,128]{3,2,1,0:T(1,128)} %bitcast.9), channel_id=1, replica_groups=mesh['seq'=64,'ch'=8] {'seq'}, dimensions={0} | all-to-all | bytes 589824 | tf_op jit(solution)/shard_map/all_to_all | solution.py:277
  43.6 0.0 copy-done.7
  43.6 0.0 copy-done.8
  43.6 0.0 copy-done
  43.6 0.0 copy-done.1
  43.6 0.0 copy-done.6
  43.6 1.1 %shard_map.138 = (f32[512,256]{1,0:T(8,128)S(1)}, f32[8,16,128]{2,1,0:T(8,128)S(1)}) custom-call(f32[576,128]{1,0:T(8,128)S(1)} %bitcast.8, bf16[128,192]{1,0:T(8,128)(2,1)S(1)} %copy-done.7, f32[64,256]{1,0:T(8,128)S(1)} %copy-done.6, bf16[2,256,256]{2,1,0:T(8,128)(2,1)S(1)} %copy-done.1, bf16[2,256,256]{2,1,0:T(8,128)(2,1)S(1)} %copy-done, ...), custom_call_target="tpu_custom_call" | custom-call | tf_op jit(solution)/shard_map/pallas_call | solution.py:294
  44.7 9.7 %all_to_all.16.side_ref = f32[8,16,128]{2,1,0:T(8,128)S(1)} all-to-all(f32[8,16,128]{2,1,0:T(8,128)S(1)} %get-tuple-element.13), channel_id=1, replica_groups=mesh['seq'=64,'ch'=8] {'ch'}, dimensions={0} | all-to-all | bytes 131072 | tf_op jit(solution)/shard_map/all_to_all | solution.py:301
  54.4 1.2 %shard_map.139 = f32[576,128]{1,0:T(8,128)S(1)} custom-call(f32[512,256]{1,0:T(8,128)S(1)} %get-tuple-element.12.spec_ref, f32[8,16,128]{2,1,0:T(8,128)S(1)} %all_to_all.16.side_ref, bf16[128,192]{1,0:T(8,128)(2,1)S(1)} %copy-done.7, f32[64,256]{1,0:T(8,128)S(1)} %copy-done.6, bf16[2,256,256]{2,1,0:T(8,128)(2,1)S(1)} %copy-done.1, ...), custom_call_target="tpu_custom_call" | custom-call | tf_op jit(solution)/shard_map/pallas_call | solution.py:302
  55.6 0.0 copy-start.2
  55.6 0.0 copy-start.3
  55.6 0.0 copy-start.4
  55.6 0.0 copy-start.5
  55.6 28.6 %all_to_all.17 = f32[64,9,1,128]{3,2,1,0:T(1,128)S(1)} all-to-all(f32[64,9,1,128]{3,2,1,0:T(1,128)S(1)} %bitcast.7), channel_id=1, replica_groups=mesh['seq'=64,'ch'=8] {'seq'}, dimensions={0} | all-to-all | bytes 589824 | tf_op jit(solution)/shard_map/all_to_all | solution.py:277
  84.2 0.0 copy-done.2
  84.2 0.0 copy-done.3
  84.2 0.0 copy-done.4
  84.2 0.8 shard_map.140
  (1 shorter events, 0.0 us)
Async XLA Ops:
  0.6 42.9 %copy-start.7 = (bf16[128,192]{1,0:T(8,128)(2,1)S(1)}, bf16[128,192]{1,0:T(8,128)(2,1)}, u32[]{:S(2)}) copy-start(bf16[128,192]{1,0:T(8,128)(2,1)} %constant.10.clone.first_ref) | copy-start | bytes 147460
  0.6 42.9 %copy-start.8 = (bf16[64,384]{1,0:T(8,128)(2,1)S(1)}, bf16[64,384]{1,0:T(8,128)(2,1)}, u32[]{:S(2)}) copy-start(bf16[64,384]{1,0:T(8,128)(2,1)} %constant.14.clone.last_ref) | copy-start | bytes 147460
  2.4 41.1 %copy-start = (bf16[2,256,256]{2,1,0:T(8,128)(2,1)S(1)}, bf16[2,256,256]{2,1,0:T(8,128)(2,1)}, u32[]{:S(2)}) copy-start(bf16[2,256,256]{2,1,0:T(8,128)(2,1)} %constant.13.clone.inverse_ref) | copy-start | bytes 786436
  2.4 41.1 %copy-start.1 = (bf16[2,256,256]{2,1,0:T(8,128)(2,1)S(1)}, bf16[2,256,256]{2,1,0:T(8,128)(2,1)}, u32[]{:S(2)}) copy-start(bf16[2,256,256]{2,1,0:T(8,128)(2,1)} %constant.12.clone.forward_ref) | copy-start | bytes 786436
  2.5 41.1 %copy-start.6 = (f32[64,256]{1,0:T(8,128)S(1)}, f32[64,256]{1,0:T(8,128)}, u32[]{:S(2)}) copy-start(f32[64,256]{1,0:T(8,128)} %constant.11.clone.twiddle_ref) | copy-start | bytes 196612
  55.6 28.7 %copy-start.2 = (bf16[256,128]{1,0:T(8,128)(2,1)S(1)}, bf16[256,128]{1,0:T(8,128)(2,1)}, u32[]{:S(2)}) copy-start(bf16[256,128]{1,0:T(8,128)(2,1)} %query_ref.1) | copy-start | bytes 196612
  55.6 28.7 %copy-start.3 = (bf16[256,128]{1,0:T(8,128)(2,1)S(1)}, bf16[256,128]{1,0:T(8,128)(2,1)}, u32[]{:S(2)}) copy-start(bf16[256,128]{1,0:T(8,128)(2,1)} %key_ref.1) | copy-start | bytes 196612
  55.6 28.6 %copy-start.4 = (bf16[256,128]{1,0:T(8,128)(2,1)S(1)}, bf16[256,128]{1,0:T(8,128)(2,1)}, u32[]{:S(2)}) copy-start(bf16[256,128]{1,0:T(8,128)(2,1)} %value_ref.1) | copy-start | bytes 196612
  55.6 28.6 %copy-start.5 = (bf16[256,128]{1,0:T(8,128)(2,1)S(1)}, bf16[256,128]{1,0:T(8,128)(2,1)}, u32[]{:S(2)}) copy-start(bf16[256,128]{1,0:T(8,128)(2,1)} %upstream_ref.1) | copy-start | bytes 196612

commit v3 on v1

--- a/solution.py
+++ b/solution.py
@@ -121,20 +121,19 @@
     return out
 
 
-def gates_kernel(sizes, query_ref, key_ref, value_ref, filters_ref, upstream_ref, out_ref, rows_ref):
+def gates_kernel(sizes, signal_ref, grad_ref, filters_ref, out_ref):
     parts, channels, own, groups = sizes
     rows = 2 * own + 1
-    filter_count = filters_ref.shape[0] // groups
+    filter_count = filters_ref.shape[1] // groups
     share = parts // filter_count
-    rows_ref[0] = key_ref[...].astype(f32) * value_ref[...].astype(f32)
-    rows_ref[1] = upstream_ref[...].astype(f32) * query_ref[...].astype(f32)
-    for which in range(2):
+    for which, source in enumerate((signal_ref, grad_ref)):
         for j in range(own):
-            out_ref[pl.ds(which * own + j, parts, stride=rows), :] = rows_ref[
-                which, pl.ds(j, parts, stride=own), :
+            out_ref[pl.ds(which * own + j, parts, stride=rows), :] = source[
+                pl.ds(j, parts, stride=own), :
             ]
+    taps = filters_ref[...].T
     side = jnp.concatenate(
-        [filters_ref[g * filter_count : (g + 1) * filter_count, :] for g in range(groups)], axis=1
+        [taps[g * filter_count : (g + 1) * filter_count, :] for g in range(groups)], axis=1
     )
     for i in range(share):
         out_ref[pl.ds(2 * own + rows * i, filter_count, stride=rows * share), :] = side
@@ -205,7 +204,7 @@
 ):
     parts, channels, own, groups = sizes
     rows = 2 * own + 1
-    filter_count = grad_filters_ref.shape[0] // groups
+    filter_count = grad_filters_ref.shape[1] // groups
     share = parts // filter_count
     for which in range(2):
         for j in range(own):
@@ -223,19 +222,19 @@
         term = y_ref[pl.ds(2 * own + rows * i, filter_count, stride=rows * share), :]
         side = term if side is None else side + term
     block = side.shape[1] // groups
-    for g in range(groups):
-        grad_filters_ref[g * filter_count : (g + 1) * filter_count, :] = side[
-            :, g * block : (g + 1) * block
-        ]
-
-
-def call(kernel, out_shape, scratch=()):
+    grad_filters_ref[...] = jnp.concatenate(
+        [side[:, g * block : (g + 1) * block] for g in range(groups)], axis=0
+    ).T
+
+
+def call(kernel, out_shape, scratch=(), grant=32, **specs):
     return pl.pallas_call(
         kernel,
         out_shape=out_shape,
         out_specs=jax.tree.map(lambda _: vmem, out_shape),
         scratch_shapes=scratch,
-        compiler_params=pltpu.CompilerParams(vmem_limit_bytes=32 * 1024 * 1024),
+        **specs,
+        compiler_params=pltpu.CompilerParams(vmem_limit_bytes=grant * 1024 * 1024),
     )
 
 
@@ -258,11 +257,11 @@
         return block.reshape(parts * rows, width)
 
     shape = jax.ShapeDtypeStruct
-    packed = call(
-        functools.partial(gates_kernel, sizes),
-        shape((parts * rows, width), f32),
-        [pltpu.VMEM((2, channels, width), f32)],
-    )(gate_query, gate_key, gate_value, filters, upstream)
+    signal = gate_key.astype(f32) * gate_value.astype(f32)
+    grad_gate = upstream.astype(f32) * gate_query.astype(f32)
+    packed = call(functools.partial(gates_kernel, sizes), shape((parts * rows, width), f32))(
+        signal, grad_gate, filters.T
+    )
     packed = exchange(packed)
     spectra, side = call(
         functools.partial(spectra_kernel, sizes),
@@ -277,11 +276,12 @@
     )
     packed = exchange(packed)
     gates = shape((channels, width), bf16)
-    return call(
+    *grads, grad_filters = call(
         functools.partial(outputs_kernel, sizes),
-        (gates, gates, gates, gates, shape(filters.shape, f32)),
+        (gates, gates, gates, gates, shape(filters.shape[::-1], f32)),
         [pltpu.VMEM((2, channels, width), f32)],
     )(packed, gate_query, gate_key, gate_value, upstream)
+    return (*grads, grad_filters.T)
 
 
 def solution(mesh):

time: 87.5 us -> 84.5 us (0.966)
  local copies, waits for them, and re-layouts: 4.06 us -> 0.06 us
  other arithmetic: 0 us -> 0.97 us
    unnamed x25 -> x20, local copies, waits for them, and re-layouts: 3.39 us -> 0.06 us
    mul x0 -> x1, other arithmetic: none -> 0.97 us  [shards(): grad_gate = upstream.astype(f32) * gate_query.astype(f32)]
where the time goes in v3:
time: 84.5 us; the launch traced here: 84.2 us
  blocking collectives  79.2 us (94%)
  Pallas kernels  3.19 us (4%)
  other arithmetic  0.97 us (1%)
    all_to_all x2, blocking collectives, exchange(): lax.all_to_all(block, 'seq', split_axis=0, concat_axis=0, tiled=True)  69.5 us
    all_to_all x1, blocking collectives, shards(): side = lax.all_to_all(side, 'ch', split_axis=0, concat_axis=0, tiled=True)  9.72 us

profile of v3, /device:TPU:24, one launch (start us, length us, event | category | flops | bytes accessed | tf_op | source)
XLA Modules:
  0.0 84.2 jit_solution(1775688845990124202)
XLA Ops:
  0.6 0.0 copy-start.9
  0.6 1.0 %convert_multiply_fusion = (f32[256,128]{1,0:T(8,128)S(1)}, f32[256,128]{1,0:T(8,128)S(1)}) fusion(bf16[256,128]{1,0:T(8,128)(2,1)} %query_ref.1, bf16[256,128]{1,0:T(8,128)(2,1)} %upstream_ref.1, bf16[256,128]{1,0:T(8,128)(2,1)} %value_ref.1, bf16[256,128]{1,0:T(8,128)(2,1)} %key_ref.1), kind=kLoop, calls=%fused_computation | loop fusion | flops 196608 | bytes 524288 | tf_op jit(solution)/shard_map/mul | solution.py:261
  1.6 0.0 copy-done.9
  1.6 0.0 copy-start.7
  1.6 0.0 copy-start.8
  1.6 0.2 shard_map.137
  1.8 0.0 copy-start
  1.8 0.0 copy-start.1
  1.8 0.0 copy-start.6
  1.9 40.9 %all_to_all.15 = f32[64,9,1,128]{3,2,1,0:T(1,128)S(1)} all-to-all(f32[64,9,1,128]{3,2,1,0:T(1,128)S(1)} %bitcast.7), channel_id=1, replica_groups=mesh['seq'=64,'ch'=8] {'seq'}, dimensions={0} | all-to-all | bytes 589824 | tf_op jit(solution)/shard_map/all_to_all | solution.py:256
  42.7 0.0 copy-done.7
  42.7 0.0 copy-done.8
  42.7 0.0 copy-done.1
  42.8 0.0 copy-done.6
  42.8 1.1 %shard_map.138 = (f32[512,256]{1,0:T(8,128)S(1)}, f32[8,16,128]{2,1,0:T(8,128)S(1)}) custom-call(f32[576,128]{1,0:T(8,128)S(1)} %bitcast.9, bf16[128,192]{1,0:T(8,128)(2,1)S(1)} %copy-done.7, f32[64,256]{1,0:T(8,128)S(1)} %copy-done.6, bf16[2,256,256]{2,1,0:T(8,128)(2,1)S(1)} %copy-done.1, bf16[2,256,256]{2,1,0:T(8,128)(2,1)S(1)} %copy-done, ...), custom_call_target="tpu_custom_call" | custom-call | tf_op jit(solution)/shard_map/pallas_call | solution.py:266
  43.8 9.7 %all_to_all.16.side_ref = f32[8,16,128]{2,1,0:T(8,128)S(1)} all-to-all(f32[8,16,128]{2,1,0:T(8,128)S(1)} %get-tuple-element.13), channel_id=1, replica_groups=mesh['seq'=64,'ch'=8] {'ch'}, dimensions={0} | all-to-all | bytes 131072 | tf_op jit(solution)/shard_map/all_to_all | solution.py:273
  53.6 1.2 %shard_map.139 = f32[576,128]{1,0:T(8,128)S(1)} custom-call(f32[512,256]{1,0:T(8,128)S(1)} %get-tuple-element.12.spec_ref, f32[8,16,128]{2,1,0:T(8,128)S(1)} %all_to_all.16.side_ref, bf16[128,192]{1,0:T(8,128)(2,1)S(1)} %copy-done.7, f32[64,256]{1,0:T(8,128)S(1)} %copy-done.6, bf16[2,256,256]{2,1,0:T(8,128)(2,1)S(1)} %copy-done.1, ...), custom_call_target="tpu_custom_call" | custom-call | tf_op jit(solution)/shard_map/pallas_call | solution.py:274
  54.7 0.0 copy-start.2
  54.8 0.0 copy-start.3
  54.8 0.0 copy-start.4
  54.8 0.0 copy-start.5
  54.8 28.6 %all_to_all.17 = f32[64,9,1,128]{3,2,1,0:T(1,128)S(1)} all-to-all(f32[64,9,1,128]{3,2,1,0:T(1,128)S(1)} %bitcast.8), channel_id=1, replica_groups=mesh['seq'=64,'ch'=8] {'seq'}, dimensions={0} | all-to-all | bytes 589824 | tf_op jit(solution)/shard_map/all_to_all | solution.py:256
  83.4 0.0 copy-done.5
  83.4 0.8 shard_map.140
  (4 shorter events, 0.0 us)
Async XLA Ops:
  0.6 1.0 %copy-start.9 = (f32[128,16]{0,1:T(8,128)S(1)}, f32[128,16]{0,1:T(8,128)}, u32[]{:S(2)}) copy-start(f32[128,16]{0,1:T(8,128)} %param.13) | copy-start | bytes 24580
  1.6 41.1 %copy-start.7 = (bf16[128,192]{1,0:T(8,128)(2,1)S(1)}, bf16[128,192]{1,0:T(8,128)(2,1)}, u32[]{:S(2)}) copy-start(bf16[128,192]{1,0:T(8,128)(2,1)} %constant.10.clone.first_ref) | copy-start | bytes 147460
  1.6 41.1 %copy-start.8 = (bf16[64,384]{1,0:T(8,128)(2,1)S(1)}, bf16[64,384]{1,0:T(8,128)(2,1)}, u32[]{:S(2)}) copy-start(bf16[64,384]{1,0:T(8,128)(2,1)} %constant.14.clone.last_ref) | copy-start | bytes 147460
  1.8 40.9 %copy-start = (bf16[2,256,256]{2,1,0:T(8,128)(2,1)S(1)}, bf16[2,256,256]{2,1,0:T(8,128)(2,1)}, u32[]{:S(2)}) copy-start(bf16[2,256,256]{2,1,0:T(8,128)(2,1)} %constant.13.clone.inverse_ref) | copy-start | bytes 786436
  1.8 40.9 %copy-start.1 = (bf16[2,256,256]{2,1,0:T(8,128)(2,1)S(1)}, bf16[2,256,256]{2,1,0:T(8,128)(2,1)}, u32[]{:S(2)}) copy-start(bf16[2,256,256]{2,1,0:T(8,128)(2,1)} %constant.12.clone.forward_ref) | copy-start | bytes 786436
  1.8 40.9 %copy-start.6 = (f32[64,256]{1,0:T(8,128)S(1)}, f32[64,256]{1,0:T(8,128)}, u32[]{:S(2)}) copy-start(f32[64,256]{1,0:T(8,128)} %constant.11.clone.twiddle_ref) | copy-start | bytes 196612
  54.7 28.7 %copy-start.2 = (bf16[256,128]{1,0:T(8,128)(2,1)S(1)}, bf16[256,128]{1,0:T(8,128)(2,1)}, u32[]{:S(2)}) copy-start(bf16[256,128]{1,0:T(8,128)(2,1)} %query_ref.1) | copy-start | bytes 196612
  54.8 28.6 %copy-start.3 = (bf16[256,128]{1,0:T(8,128)(2,1)S(1)}, bf16[256,128]{1,0:T(8,128)(2,1)}, u32[]{:S(2)}) copy-start(bf16[256,128]{1,0:T(8,128)(2,1)} %upstream_ref.1) | copy-start | bytes 196612
  54.8 28.6 %copy-start.4 = (bf16[256,128]{1,0:T(8,128)(2,1)S(1)}, bf16[256,128]{1,0:T(8,128)(2,1)}, u32[]{:S(2)}) copy-start(bf16[256,128]{1,0:T(8,128)(2,1)} %value_ref.1) | copy-start | bytes 196612
  54.8 28.6 %copy-start.5 = (bf16[256,128]{1,0:T(8,128)(2,1)S(1)}, bf16[256,128]{1,0:T(8,128)(2,1)}, u32[]{:S(2)}) copy-start(bf16[256,128]{1,0:T(8,128)(2,1)} %key_ref.1) | copy-start | bytes 196612

commit v4 on v3

--- a/solution.py
+++ b/solution.py
@@ -21,10 +21,10 @@
     return high, low
 
 
-def make_tables(parts, width):
+def make_tables(parts, width, order):
     total = parts * width
     k1 = np.arange(parts) + 0.25
-    p = np.arange(parts)
+    p = np.asarray(order)
     b = np.arange(width)
     outer = 2.0 * np.pi / parts * (k1[:, None] * p[None, :])
     first = np.concatenate([np.cos(outer), -np.sin(outer)], axis=0)
@@ -140,7 +140,7 @@
 
 
 def spectra_kernel(
-    sizes, x_ref, first_ref, twiddle_ref, forward_ref, inverse_ref, last_ref, spec_ref, out_ref
+    sizes, members, x_ref, first_ref, twiddle_ref, forward_ref, inverse_ref, last_ref, spec_ref, out_ref
 ):
     parts, channels, own, groups = sizes
     rows = 2 * own + 1
@@ -159,18 +159,23 @@
         count = parts // groups
         pieces = lane_blocks([block[a * count : (a + 1) * count] for a in range(groups)])
         for g in range(groups):
-            out_ref[g, which * count : (which + 1) * count, :] = pieces[g]
+            out_ref[g, which * count : (which + 1) * count, :] = pieces[members[g]]
 
 
 def fields_kernel(
-    sizes, tap_scale, spec_ref, side_ref, first_ref, twiddle_ref, forward_ref, inverse_ref, last_ref, out_ref
+    sizes, members, tap_scale, spec_ref, side_ref, first_ref, twiddle_ref, forward_ref, inverse_ref, last_ref, out_ref
 ):
     parts, channels, own, groups = sizes
     rows = 2 * own + 1
     count = parts // groups
     taps, grad_taps = (
         jnp.concatenate(
-            lane_blocks([side_ref[g, which * count : (which + 1) * count, :] for g in range(groups)]),
+            lane_blocks(
+                [
+                    side_ref[members.index(g), which * count : (which + 1) * count, :]
+                    for g in range(groups)
+                ]
+            ),
             axis=0,
         )
         for which in range(2)
@@ -246,14 +251,18 @@
     rows = 2 * own + 1
     sizes = (parts, channels, own, groups)
     tap_scale = 1.0 / math.sqrt(parts * width)
-    tables = make_tables(parts, width)
+    members = [(i + 5) % groups for i in range(groups)]
+    order = [16 * ((i + 2) % 4) + (i // 4 + 11) % 16 for i in range(parts)]
+    tables = make_tables(parts, width, order)
     first, twiddle, forward, inverse, last = (
         jnp.asarray(tables[name]) for name in ("first", "twiddle", "forward", "inverse", "last")
     )
 
     def exchange(block):
         block = block.reshape(parts, rows, 1, width)
-        block = lax.all_to_all(block, "seq", split_axis=0, concat_axis=0, tiled=True)
+        block = lax.all_to_all(
+            block, "seq", split_axis=0, concat_axis=0, tiled=True, axis_index_groups=[order]
+        )
         return block.reshape(parts * rows, width)
 
     shape = jax.ShapeDtypeStruct
@@ -264,14 +273,16 @@
     )
     packed = exchange(packed)
     spectra, side = call(
-        functools.partial(spectra_kernel, sizes),
+        functools.partial(spectra_kernel, sizes, members),
         (
             shape((2 * own * parts, 2 * width), f32),
             shape((groups, 2 * parts // groups, width), f32),
         ),
     )(packed, first, twiddle, forward, inverse, last)
-    side = lax.all_to_all(side, "ch", split_axis=0, concat_axis=0, tiled=True)
-    packed = call(functools.partial(fields_kernel, sizes, tap_scale), shape((parts * rows, width), f32))(
+    side = lax.all_to_all(
+        side, "ch", split_axis=0, concat_axis=0, tiled=True, axis_index_groups=[members]
+    )
+    packed = call(functools.partial(fields_kernel, sizes, members, tap_scale), shape((parts * rows, width), f32))(
         spectra, side, first, twiddle, forward, inverse, last
     )
     packed = exchange(packed)

time: 84.5 us -> 77.4 us (0.916); the launches traced: 84.2 us -> 76 us
  blocking collectives: 79.2 us -> 71 us
    all_to_all x3, blocking collectives: 79.2 us -> 71 us  [the longest x2 63.3 us: exchange(): lax.all_to_all(block, 'seq', split_axis=0, concat_axis=0, tiled=True, axi...]
where the time goes in v4:
time: 77.4 us; the launch traced here: 76 us
  blocking collectives  71 us (92%)
  Pallas kernels  3.19 us (4%)
  other arithmetic  0.97 us (1%)
    all_to_all x2, blocking collectives, exchange(): lax.all_to_all(block, 'seq', split_axis=0, concat_axis=0, tiled=True, axi...  63.3 us
    all_to_all x1, blocking collectives, shards(): lax.all_to_all(side, 'ch', split_axis=0, concat_axis=0, tiled=True, axis_...  7.67 us

profile of v4, /device:TPU:24, one launch (start us, length us, event | category | flops | bytes accessed | tf_op | source)
XLA Modules:
  0.0 76.0 jit_solution(6336222768258073020)
XLA Ops:
  0.6 0.0 copy-start.9
  0.6 1.0 %convert_multiply_fusion = (f32[256,128]{1,0:T(8,128)S(1)}, f32[256,128]{1,0:T(8,128)S(1)}) fusion(bf16[256,128]{1,0:T(8,128)(2,1)} %query_ref.1, bf16[256,128]{1,0:T(8,128)(2,1)} %upstream_ref.1, bf16[256,128]{1,0:T(8,128)(2,1)} %value_ref.1, bf16[256,128]{1,0:T(8,128)(2,1)} %key_ref.1), kind=kLoop, calls=%fused_computation | loop fusion | flops 196608 | bytes 524288 | tf_op jit(solution)/shard_map/mul | solution.py:270
  1.6 0.0 copy-done.9
  1.6 0.0 copy-start.7
  1.6 0.0 copy-start.8
  1.6 0.2 shard_map.137
  1.8 0.0 copy-start
  1.8 0.0 copy-start.1
  1.8 0.0 copy-start.6
  1.9 34.4 %all_to_all.15 = f32[64,9,1,128]{3,2,1,0:T(1,128)S(1)} all-to-all(f32[64,9,1,128]{3,2,1,0:T(1,128)S(1)} %bitcast.7), channel_id=1, replica_groups={{344,472,88,216,352,480,96,224,360,488,104,232,368,496,112,240,376,504,..., dimensions={0} | all-to-all | bytes 589824 | tf_op jit(solution)/shard_map/all_to_all | solution.py:263
  36.3 0.0 copy-done.7
  36.3 0.0 copy-done.8
  36.3 0.0 copy-done
  36.3 0.0 copy-done.1
  36.3 1.1 %shard_map.138 = (f32[512,256]{1,0:T(8,128)S(1)}, f32[8,16,128]{2,1,0:T(8,128)S(1)}) custom-call(f32[576,128]{1,0:T(8,128)S(1)} %bitcast.9, bf16[128,192]{1,0:T(8,128)(2,1)S(1)} %copy-done.7, f32[64,256]{1,0:T(8,128)S(1)} %copy-done.6, bf16[2,256,256]{2,1,0:T(8,128)(2,1)S(1)} %copy-done.1, bf16[2,256,256]{2,1,0:T(8,128)(2,1)S(1)} %copy-done, ...), custom_call_target="tpu_custom_call" | custom-call | tf_op jit(solution)/shard_map/pallas_call | solution.py:275
  37.4 7.7 %all_to_all.16.side_ref = f32[8,16,128]{2,1,0:T(8,128)S(1)} all-to-all(f32[8,16,128]{2,1,0:T(8,128)S(1)} %get-tuple-element.13), channel_id=1, replica_groups={{5,6,7,0,1,2,3,4},{13,14,15,8,9,10,11,12},{21,22,23,16,17,18,19,20},{29..., dimensions={0} | all-to-all | bytes 131072 | tf_op jit(solution)/shard_map/all_to_all | solution.py:282
  45.0 1.2 %shard_map.139 = f32[576,128]{1,0:T(8,128)S(1)} custom-call(f32[512,256]{1,0:T(8,128)S(1)} %get-tuple-element.12.spec_ref, f32[8,16,128]{2,1,0:T(8,128)S(1)} %all_to_all.16.side_ref, bf16[128,192]{1,0:T(8,128)(2,1)S(1)} %copy-done.7, f32[64,256]{1,0:T(8,128)S(1)} %copy-done.6, bf16[2,256,256]{2,1,0:T(8,128)(2,1)S(1)} %copy-done.1, ...), custom_call_target="tpu_custom_call" | custom-call | tf_op jit(solution)/shard_map/pallas_call | solution.py:285
  46.2 0.0 copy-start.2
  46.2 0.0 copy-start.3
  46.2 0.0 copy-start.4
  46.3 0.0 copy-start.5
  46.3 28.9 %all_to_all.17 = f32[64,9,1,128]{3,2,1,0:T(1,128)S(1)} all-to-all(f32[64,9,1,128]{3,2,1,0:T(1,128)S(1)} %bitcast.8), channel_id=1, replica_groups={{344,472,88,216,352,480,96,224,360,488,104,232,368,496,112,240,376,504,..., dimensions={0} | all-to-all | bytes 589824 | tf_op jit(solution)/shard_map/all_to_all | solution.py:263
  75.2 0.0 copy-done.2
  75.2 0.8 %shard_map.140 = (bf16[256,128]{1,0:T(8,128)(2,1)}, bf16[256,128]{1,0:T(8,128)(2,1)}, bf16[256,128]{1,0:T(8,128)(2,1)}, bf16[256,128]{1,0:T(8,128)(2,1)}, f32[16,128]{1,0:T(8,128)}) custom-call(f32[576,128]{1,0:T(8,128)S(1)} %bitcast.6, bf16[256,128]{1,0:T(8,128)(2,1)S(1)} %copy-done.2, bf16[256,128]{1,0:T(8,128)(2,1)S(1)} %copy-done.5, ...), custom_call_target="tpu_custom_call" | custom-call | tf_op jit(solution)/shard_map/pallas_call | solution.py:290
  (4 shorter events, 0.0 us)
Async XLA Ops:
  0.6 1.0 %copy-start.9 = (f32[128,16]{0,1:T(8,128)S(1)}, f32[128,16]{0,1:T(8,128)}, u32[]{:S(2)}) copy-start(f32[128,16]{0,1:T(8,128)} %param.13) | copy-start | bytes 24580
  1.6 34.6 %copy-start.7 = (bf16[128,192]{1,0:T(8,128)(2,1)S(1)}, bf16[128,192]{1,0:T(8,128)(2,1)}, u32[]{:S(2)}) copy-start(bf16[128,192]{1,0:T(8,128)(2,1)} %constant.10.clone.first_ref) | copy-start | bytes 147460
  1.6 34.6 %copy-start.8 = (bf16[64,384]{1,0:T(8,128)(2,1)S(1)}, bf16[64,384]{1,0:T(8,128)(2,1)}, u32[]{:S(2)}) copy-start(bf16[64,384]{1,0:T(8,128)(2,1)} %constant.14.clone.last_ref) | copy-start | bytes 147460
  1.8 34.5 %copy-start = (bf16[2,256,256]{2,1,0:T(8,128)(2,1)S(1)}, bf16[2,256,256]{2,1,0:T(8,128)(2,1)}, u32[]{:S(2)}) copy-start(bf16[2,256,256]{2,1,0:T(8,128)(2,1)} %constant.13.clone.inverse_ref) | copy-start | bytes 786436
  1.8 34.4 %copy-start.1 = (bf16[2,256,256]{2,1,0:T(8,128)(2,1)S(1)}, bf16[2,256,256]{2,1,0:T(8,128)(2,1)}, u32[]{:S(2)}) copy-start(bf16[2,256,256]{2,1,0:T(8,128)(2,1)} %constant.12.clone.forward_ref) | copy-start | bytes 786436
  1.8 34.4 %copy-start.6 = (f32[64,256]{1,0:T(8,128)S(1)}, f32[64,256]{1,0:T(8,128)}, u32[]{:S(2)}) copy-start(f32[64,256]{1,0:T(8,128)} %constant.11.clone.twiddle_ref) | copy-start | bytes 196612
  46.2 28.9 %copy-start.2 = (bf16[256,128]{1,0:T(8,128)(2,1)S(1)}, bf16[256,128]{1,0:T(8,128)(2,1)}, u32[]{:S(2)}) copy-start(bf16[256,128]{1,0:T(8,128)(2,1)} %query_ref.1) | copy-start | bytes 196612
  46.2 28.9 %copy-start.3 = (bf16[256,128]{1,0:T(8,128)(2,1)S(1)}, bf16[256,128]{1,0:T(8,128)(2,1)}, u32[]{:S(2)}) copy-start(bf16[256,128]{1,0:T(8,128)(2,1)} %upstream_ref.1) | copy-start | bytes 196612
  46.2 28.9 %copy-start.4 = (bf16[256,128]{1,0:T(8,128)(2,1)S(1)}, bf16[256,128]{1,0:T(8,128)(2,1)}, u32[]{:S(2)}) copy-start(bf16[256,128]{1,0:T(8,128)(2,1)} %value_ref.1) | copy-start | bytes 196612
  46.3 28.9 %copy-start.5 = (bf16[256,128]{1,0:T(8,128)(2,1)S(1)}, bf16[256,128]{1,0:T(8,128)(2,1)}, u32[]{:S(2)}) copy-start(bf16[256,128]{1,0:T(8,128)(2,1)} %key_ref.1) | copy-start | bytes 196612

commit v5 on v4

--- a/solution.py
+++ b/solution.py
@@ -252,7 +252,7 @@
     sizes = (parts, channels, own, groups)
     tap_scale = 1.0 / math.sqrt(parts * width)
     members = [(i + 5) % groups for i in range(groups)]
-    order = [16 * ((i + 2) % 4) + (i // 4 + 11) % 16 for i in range(parts)]
+    order = [16 * ((i + 2) % 4) + (11 - i // 4) % 16 for i in range(parts)]
     tables = make_tables(parts, width, order)
     first, twiddle, forward, inverse, last = (
         jnp.asarray(tables[name]) for name in ("first", "twiddle", "forward", "inverse", "last")

time: 77.4 us -> 77.3 us (level); the launches traced: 76 us -> 77 us
  blocking collectives: 71 us -> 72 us
    all_to_all x2, blocking collectives: 63.3 us -> 64.4 us  [exchange(): lax.all_to_all(block, 'seq', split_axis=0, concat_axis=0, tiled=True, axi...]
where the time goes in v5:
time: 77.3 us; the launch traced here: 77 us
  blocking collectives  72 us (93%)
  Pallas kernels  3.19 us (4%)
  other arithmetic  0.97 us (1%)
    all_to_all x2, blocking collectives, exchange(): lax.all_to_all(block, 'seq', split_axis=0, concat_axis=0, tiled=True, axi...  64.4 us
    all_to_all x1, blocking collectives, shards(): lax.all_to_all(side, 'ch', split_axis=0, concat_axis=0, tiled=True, axis_...  7.67 us

profile of v5, /device:TPU:24, one launch (start us, length us, event | category | flops | bytes accessed | tf_op | source)
XLA Modules:
  0.0 77.0 jit_solution(6077813648179239512)
XLA Ops:
  0.6 0.0 copy-start.9
  0.6 1.0 %convert_multiply_fusion = (f32[256,128]{1,0:T(8,128)S(1)}, f32[256,128]{1,0:T(8,128)S(1)}) fusion(bf16[256,128]{1,0:T(8,128)(2,1)} %query_ref.1, bf16[256,128]{1,0:T(8,128)(2,1)} %upstream_ref.1, bf16[256,128]{1,0:T(8,128)(2,1)} %value_ref.1, bf16[256,128]{1,0:T(8,128)(2,1)} %key_ref.1), kind=kLoop, calls=%fused_computation | loop fusion | flops 196608 | bytes 524288 | tf_op jit(solution)/shard_map/mul | solution.py:270
  1.6 0.0 copy-done.9
  1.6 0.0 copy-start.7
  1.6 0.0 copy-start.8
  1.6 0.2 shard_map.137
  1.8 0.0 copy-start
  1.8 0.0 copy-start.1
  1.8 0.0 copy-start.6
  1.9 35.5 %all_to_all.15 = f32[64,9,1,128]{3,2,1,0:T(1,128)S(1)} all-to-all(f32[64,9,1,128]{3,2,1,0:T(1,128)S(1)} %bitcast.7), channel_id=1, replica_groups={{344,472,88,216,336,464,80,208,328,456,72,200,320,448,64,192,312,440,56..., dimensions={0} | all-to-all | bytes 589824 | tf_op jit(solution)/shard_map/all_to_all | solution.py:263
  37.4 0.0 copy-done.7
  37.4 0.0 copy-done.8
  37.4 0.0 copy-done
  37.4 0.0 copy-done.1
  37.4 1.1 %shard_map.138 = (f32[512,256]{1,0:T(8,128)S(1)}, f32[8,16,128]{2,1,0:T(8,128)S(1)}) custom-call(f32[576,128]{1,0:T(8,128)S(1)} %bitcast.9, bf16[128,192]{1,0:T(8,128)(2,1)S(1)} %copy-done.7, f32[64,256]{1,0:T(8,128)S(1)} %copy-done.6, bf16[2,256,256]{2,1,0:T(8,128)(2,1)S(1)} %copy-done.1, bf16[2,256,256]{2,1,0:T(8,128)(2,1)S(1)} %copy-done, ...), custom_call_target="tpu_custom_call" | custom-call | tf_op jit(solution)/shard_map/pallas_call | solution.py:275
  38.5 7.7 %all_to_all.16.side_ref = f32[8,16,128]{2,1,0:T(8,128)S(1)} all-to-all(f32[8,16,128]{2,1,0:T(8,128)S(1)} %get-tuple-element.13), channel_id=1, replica_groups={{5,6,7,0,1,2,3,4},{13,14,15,8,9,10,11,12},{21,22,23,16,17,18,19,20},{29..., dimensions={0} | all-to-all | bytes 131072 | tf_op jit(solution)/shard_map/all_to_all | solution.py:282
  46.1 1.2 %shard_map.139 = f32[576,128]{1,0:T(8,128)S(1)} custom-call(f32[512,256]{1,0:T(8,128)S(1)} %get-tuple-element.12.spec_ref, f32[8,16,128]{2,1,0:T(8,128)S(1)} %all_to_all.16.side_ref, bf16[128,192]{1,0:T(8,128)(2,1)S(1)} %copy-done.7, f32[64,256]{1,0:T(8,128)S(1)} %copy-done.6, bf16[2,256,256]{2,1,0:T(8,128)(2,1)S(1)} %copy-done.1, ...), custom_call_target="tpu_custom_call" | custom-call | tf_op jit(solution)/shard_map/pallas_call | solution.py:285
  47.3 0.0 copy-start.2
  47.3 0.0 copy-start.3
  47.3 0.0 copy-start.4
  47.4 0.0 copy-start.5
  47.4 28.9 %all_to_all.17 = f32[64,9,1,128]{3,2,1,0:T(1,128)S(1)} all-to-all(f32[64,9,1,128]{3,2,1,0:T(1,128)S(1)} %bitcast.8), channel_id=1, replica_groups={{344,472,88,216,336,464,80,208,328,456,72,200,320,448,64,192,312,440,56..., dimensions={0} | all-to-all | bytes 589824 | tf_op jit(solution)/shard_map/all_to_all | solution.py:263
  76.2 0.0 copy-done.5
  76.2 0.8 %shard_map.140 = (bf16[256,128]{1,0:T(8,128)(2,1)}, bf16[256,128]{1,0:T(8,128)(2,1)}, bf16[256,128]{1,0:T(8,128)(2,1)}, bf16[256,128]{1,0:T(8,128)(2,1)}, f32[16,128]{1,0:T(8,128)}) custom-call(f32[576,128]{1,0:T(8,128)S(1)} %bitcast.6, bf16[256,128]{1,0:T(8,128)(2,1)S(1)} %copy-done.2, bf16[256,128]{1,0:T(8,128)(2,1)S(1)} %copy-done.5, ...), custom_call_target="tpu_custom_call" | custom-call | tf_op jit(solution)/shard_map/pallas_call | solution.py:290
  (4 shorter events, 0.0 us)
Async XLA Ops:
  0.6 1.0 %copy-start.9 = (f32[128,16]{0,1:T(8,128)S(1)}, f32[128,16]{0,1:T(8,128)}, u32[]{:S(2)}) copy-start(f32[128,16]{0,1:T(8,128)} %param.13) | copy-start | bytes 24580
  1.6 35.7 %copy-start.7 = (bf16[128,192]{1,0:T(8,128)(2,1)S(1)}, bf16[128,192]{1,0:T(8,128)(2,1)}, u32[]{:S(2)}) copy-start(bf16[128,192]{1,0:T(8,128)(2,1)} %constant.10.clone.first_ref) | copy-start | bytes 147460
  1.6 35.7 %copy-start.8 = (bf16[64,384]{1,0:T(8,128)(2,1)S(1)}, bf16[64,384]{1,0:T(8,128)(2,1)}, u32[]{:S(2)}) copy-start(bf16[64,384]{1,0:T(8,128)(2,1)} %constant.14.clone.last_ref) | copy-start | bytes 147460
  1.8 35.6 %copy-start = (bf16[2,256,256]{2,1,0:T(8,128)(2,1)S(1)}, bf16[2,256,256]{2,1,0:T(8,128)(2,1)}, u32[]{:S(2)}) copy-start(bf16[2,256,256]{2,1,0:T(8,128)(2,1)} %constant.13.clone.inverse_ref) | copy-start | bytes 786436
  1.8 35.5 %copy-start.1 = (bf16[2,256,256]{2,1,0:T(8,128)(2,1)S(1)}, bf16[2,256,256]{2,1,0:T(8,128)(2,1)}, u32[]{:S(2)}) copy-start(bf16[2,256,256]{2,1,0:T(8,128)(2,1)} %constant.12.clone.forward_ref) | copy-start | bytes 786436
  1.8 35.5 %copy-start.6 = (f32[64,256]{1,0:T(8,128)S(1)}, f32[64,256]{1,0:T(8,128)}, u32[]{:S(2)}) copy-start(f32[64,256]{1,0:T(8,128)} %constant.11.clone.twiddle_ref) | copy-start | bytes 196612
  47.3 28.9 %copy-start.2 = (bf16[256,128]{1,0:T(8,128)(2,1)S(1)}, bf16[256,128]{1,0:T(8,128)(2,1)}, u32[]{:S(2)}) copy-start(bf16[256,128]{1,0:T(8,128)(2,1)} %query_ref.1) | copy-start | bytes 196612
  47.3 28.9 %copy-start.3 = (bf16[256,128]{1,0:T(8,128)(2,1)S(1)}, bf16[256,128]{1,0:T(8,128)(2,1)}, u32[]{:S(2)}) copy-start(bf16[256,128]{1,0:T(8,128)(2,1)} %upstream_ref.1) | copy-start | bytes 196612
  47.3 28.9 %copy-start.4 = (bf16[256,128]{1,0:T(8,128)(2,1)S(1)}, bf16[256,128]{1,0:T(8,128)(2,1)}, u32[]{:S(2)}) copy-start(bf16[256,128]{1,0:T(8,128)(2,1)} %value_ref.1) | copy-start | bytes 196612
  47.4 28.9 %copy-start.5 = (bf16[256,128]{1,0:T(8,128)(2,1)S(1)}, bf16[256,128]{1,0:T(8,128)(2,1)}, u32[]{:S(2)}) copy-start(bf16[256,128]{1,0:T(8,128)(2,1)} %key_ref.1) | copy-start | bytes 196612

commit v6 on v4

--- a/solution.py
+++ b/solution.py
@@ -110,15 +110,17 @@
     count = len(pieces)
     block = pieces[0].shape[1] // count
     lane = lax.broadcasted_iota(jnp.int32, pieces[0].shape, 1) // block
-    out = []
-    for c in range(count):
-        total = pieces[0] if c == 0 else pltpu.roll(pieces[0], (-c) % count * block, 1)
-        for a in range(1, count):
-            shift = (a - c) % count * block
-            moved = pieces[a] if shift == 0 else pltpu.roll(pieces[a], shift, 1)
-            total = jnp.where(lane == a, moved, total)
-        out.append(total)
-    return out
+    pieces = list(pieces)
+    half = count // 2
+    while half:
+        upper = lane // half % 2 == 1
+        for a in range(count):
+            if a // half % 2 == 0:
+                low, high = pieces[a], pieces[a + half]
+                pieces[a] = jnp.where(upper, pltpu.roll(high, half * block, 1), low)
+                pieces[a + half] = jnp.where(upper, high, pltpu.roll(low, (count - half) * block, 1))
+        half //= 2
+    return pieces
 
 
 def gates_kernel(sizes, signal_ref, grad_ref, filters_ref, out_ref):

time: 77.4 us -> 77.6 us (level)
  no operation moved by 1% of the time
where the time goes in v6:
time: 77.6 us; the launch traced here: 76.1 us
  blocking collectives  71 us (91%)
  Pallas kernels  3.36 us (4%)
  other arithmetic  0.97 us (1%)
    all_to_all x2, blocking collectives, exchange(): lax.all_to_all(block, 'seq', split_axis=0, concat_axis=0, tiled=True, axi...  63.3 us
    all_to_all x1, blocking collectives, shards(): lax.all_to_all(side, 'ch', split_axis=0, concat_axis=0, tiled=True, axis_...  7.67 us

profile of v6, /device:TPU:24, one launch (start us, length us, event | category | flops | bytes accessed | tf_op | source)
XLA Modules:
  0.0 76.1 jit_solution(3145559405279760690)
XLA Ops:
  0.6 0.0 copy-start.9
  0.6 1.0 %convert_multiply_fusion = (f32[256,128]{1,0:T(8,128)S(1)}, f32[256,128]{1,0:T(8,128)S(1)}) fusion(bf16[256,128]{1,0:T(8,128)(2,1)} %query_ref.1, bf16[256,128]{1,0:T(8,128)(2,1)} %upstream_ref.1, bf16[256,128]{1,0:T(8,128)(2,1)} %value_ref.1, bf16[256,128]{1,0:T(8,128)(2,1)} %key_ref.1), kind=kLoop, calls=%fused_computation | loop fusion | flops 196608 | bytes 524288 | tf_op jit(solution)/shard_map/mul | solution.py:272
  1.6 0.0 copy-done.9
  1.6 0.0 copy-start.7
  1.6 0.0 copy-start.8
  1.6 0.2 shard_map.137
  1.8 0.0 copy-start
  1.8 0.0 copy-start.1
  1.8 0.0 copy-start.6
  1.9 34.4 %all_to_all.15 = f32[64,9,1,128]{3,2,1,0:T(1,128)S(1)} all-to-all(f32[64,9,1,128]{3,2,1,0:T(1,128)S(1)} %bitcast.7), channel_id=1, replica_groups={{344,472,88,216,352,480,96,224,360,488,104,232,368,496,112,240,376,504,..., dimensions={0} | all-to-all | bytes 589824 | tf_op jit(solution)/shard_map/all_to_all | solution.py:265
  36.3 0.0 copy-done.7
  36.3 0.0 copy-done.8
  36.3 0.0 copy-done
  36.3 0.0 copy-done.1
  36.3 0.0 copy-done.6
  36.3 1.2 %shard_map.138 = (f32[512,256]{1,0:T(8,128)S(1)}, f32[8,16,128]{2,1,0:T(8,128)S(1)}) custom-call(f32[576,128]{1,0:T(8,128)S(1)} %bitcast.9, bf16[128,192]{1,0:T(8,128)(2,1)S(1)} %copy-done.7, f32[64,256]{1,0:T(8,128)S(1)} %copy-done.6, bf16[2,256,256]{2,1,0:T(8,128)(2,1)S(1)} %copy-done.1, bf16[2,256,256]{2,1,0:T(8,128)(2,1)S(1)} %copy-done, ...), custom_call_target="tpu_custom_call" | custom-call | tf_op jit(solution)/shard_map/pallas_call | solution.py:277
  37.5 7.7 %all_to_all.16.side_ref = f32[8,16,128]{2,1,0:T(8,128)S(1)} all-to-all(f32[8,16,128]{2,1,0:T(8,128)S(1)} %get-tuple-element.13), channel_id=1, replica_groups={{5,6,7,0,1,2,3,4},{13,14,15,8,9,10,11,12},{21,22,23,16,17,18,19,20},{29..., dimensions={0} | all-to-all | bytes 131072 | tf_op jit(solution)/shard_map/all_to_all | solution.py:284
  45.1 1.3 %shard_map.139 = f32[576,128]{1,0:T(8,128)S(1)} custom-call(f32[512,256]{1,0:T(8,128)S(1)} %get-tuple-element.12.spec_ref, f32[8,16,128]{2,1,0:T(8,128)S(1)} %all_to_all.16.side_ref, bf16[128,192]{1,0:T(8,128)(2,1)S(1)} %copy-done.7, f32[64,256]{1,0:T(8,128)S(1)} %copy-done.6, bf16[2,256,256]{2,1,0:T(8,128)(2,1)S(1)} %copy-done.1, ...), custom_call_target="tpu_custom_call" | custom-call | tf_op jit(solution)/shard_map/pallas_call | solution.py:287
  46.4 0.0 copy-start.2
  46.4 0.0 copy-start.3
  46.4 0.0 copy-start.4
  46.4 0.0 copy-start.5
  46.4 28.9 %all_to_all.17 = f32[64,9,1,128]{3,2,1,0:T(1,128)S(1)} all-to-all(f32[64,9,1,128]{3,2,1,0:T(1,128)S(1)} %bitcast.8), channel_id=1, replica_groups={{344,472,88,216,352,480,96,224,360,488,104,232,368,496,112,240,376,504,..., dimensions={0} | all-to-all | bytes 589824 | tf_op jit(solution)/shard_map/all_to_all | solution.py:265
  75.4 0.8 %shard_map.140 = (bf16[256,128]{1,0:T(8,128)(2,1)}, bf16[256,128]{1,0:T(8,128)(2,1)}, bf16[256,128]{1,0:T(8,128)(2,1)}, bf16[256,128]{1,0:T(8,128)(2,1)}, f32[16,128]{1,0:T(8,128)}) custom-call(f32[576,128]{1,0:T(8,128)S(1)} %bitcast.6, bf16[256,128]{1,0:T(8,128)(2,1)S(1)} %copy-done.2, bf16[256,128]{1,0:T(8,128)(2,1)S(1)} %copy-done.5, ...), custom_call_target="tpu_custom_call" | custom-call | tf_op jit(solution)/shard_map/pallas_call | solution.py:292
  (4 shorter events, 0.0 us)
Async XLA Ops:
  0.6 1.0 %copy-start.9 = (f32[128,16]{0,1:T(8,128)S(1)}, f32[128,16]{0,1:T(8,128)}, u32[]{:S(2)}) copy-start(f32[128,16]{0,1:T(8,128)} %param.13) | copy-start | bytes 24580
  1.6 34.6 %copy-start.7 = (bf16[128,192]{1,0:T(8,128)(2,1)S(1)}, bf16[128,192]{1,0:T(8,128)(2,1)}, u32[]{:S(2)}) copy-start(bf16[128,192]{1,0:T(8,128)(2,1)} %constant.10.clone.first_ref) | copy-start | bytes 147460
  1.6 34.6 %copy-start.8 = (bf16[64,384]{1,0:T(8,128)(2,1)S(1)}, bf16[64,384]{1,0:T(8,128)(2,1)}, u32[]{:S(2)}) copy-start(bf16[64,384]{1,0:T(8,128)(2,1)} %constant.14.clone.last_ref) | copy-start | bytes 147460
  1.8 34.5 %copy-start = (bf16[2,256,256]{2,1,0:T(8,128)(2,1)S(1)}, bf16[2,256,256]{2,1,0:T(8,128)(2,1)}, u32[]{:S(2)}) copy-start(bf16[2,256,256]{2,1,0:T(8,128)(2,1)} %constant.13.clone.inverse_ref) | copy-start | bytes 786436
  1.8 34.4 %copy-start.1 = (bf16[2,256,256]{2,1,0:T(8,128)(2,1)S(1)}, bf16[2,256,256]{2,1,0:T(8,128)(2,1)}, u32[]{:S(2)}) copy-start(bf16[2,256,256]{2,1,0:T(8,128)(2,1)} %constant.12.clone.forward_ref) | copy-start | bytes 786436
  1.8 34.4 %copy-start.6 = (f32[64,256]{1,0:T(8,128)S(1)}, f32[64,256]{1,0:T(8,128)}, u32[]{:S(2)}) copy-start(f32[64,256]{1,0:T(8,128)} %constant.11.clone.twiddle_ref) | copy-start | bytes 196612
  46.4 28.9 %copy-start.2 = (bf16[256,128]{1,0:T(8,128)(2,1)S(1)}, bf16[256,128]{1,0:T(8,128)(2,1)}, u32[]{:S(2)}) copy-start(bf16[256,128]{1,0:T(8,128)(2,1)} %query_ref.1) | copy-start | bytes 196612
  46.4 28.9 %copy-start.3 = (bf16[256,128]{1,0:T(8,128)(2,1)S(1)}, bf16[256,128]{1,0:T(8,128)(2,1)}, u32[]{:S(2)}) copy-start(bf16[256,128]{1,0:T(8,128)(2,1)} %upstream_ref.1) | copy-start | bytes 196612
  46.4 28.9 %copy-start.4 = (bf16[256,128]{1,0:T(8,128)(2,1)S(1)}, bf16[256,128]{1,0:T(8,128)(2,1)}, u32[]{:S(2)}) copy-start(bf16[256,128]{1,0:T(8,128)(2,1)} %value_ref.1) | copy-start | bytes 196612
  46.4 28.9 %copy-start.5 = (bf16[256,128]{1,0:T(8,128)(2,1)S(1)}, bf16[256,128]{1,0:T(8,128)(2,1)}, u32[]{:S(2)}) copy-start(bf16[256,128]{1,0:T(8,128)(2,1)} %key_ref.1) | copy-start | bytes 196612

commit v7 on v5

--- a/solution.py
+++ b/solution.py
@@ -252,7 +252,7 @@
     sizes = (parts, channels, own, groups)
     tap_scale = 1.0 / math.sqrt(parts * width)
     members = [(i + 5) % groups for i in range(groups)]
-    order = [16 * ((i + 2) % 4) + (11 - i // 4) % 16 for i in range(parts)]
+    order = [43] + [i for i in range(parts) if i != 43]
     tables = make_tables(parts, width, order)
     first, twiddle, forward, inverse, last = (
         jnp.asarray(tables[name]) for name in ("first", "twiddle", "forward", "inverse", "last")

time: 77.3 us -> 77.4 us (level)
  no operation moved by 1% of the time
where the time goes in v7:
time: 77.4 us; the launch traced here: 76.5 us
  blocking collectives  71.5 us (92%)
  Pallas kernels  3.19 us (4%)
  other arithmetic  0.97 us (1%)
    all_to_all x2, blocking collectives, exchange(): lax.all_to_all(block, 'seq', split_axis=0, concat_axis=0, tiled=True, axi...  63.8 us
    all_to_all x1, blocking collectives, shards(): lax.all_to_all(side, 'ch', split_axis=0, concat_axis=0, tiled=True, axis_...  7.67 us

profile of v7, /device:TPU:24, one launch (start us, length us, event | category | flops | bytes accessed | tf_op | source)
XLA Modules:
  0.0 76.5 jit_solution(10475535853860872455)
XLA Ops:
  0.6 0.0 copy-start.9
  0.6 1.0 %convert_multiply_fusion = (f32[256,128]{1,0:T(8,128)S(1)}, f32[256,128]{1,0:T(8,128)S(1)}) fusion(bf16[256,128]{1,0:T(8,128)(2,1)} %query_ref.1, bf16[256,128]{1,0:T(8,128)(2,1)} %upstream_ref.1, bf16[256,128]{1,0:T(8,128)(2,1)} %value_ref.1, bf16[256,128]{1,0:T(8,128)(2,1)} %key_ref.1), kind=kLoop, calls=%fused_computation | loop fusion | flops 196608 | bytes 524288 | tf_op jit(solution)/shard_map/mul | solution.py:270
  1.6 0.0 copy-done.9
  1.6 0.0 copy-start.7
  1.6 0.0 copy-start.8
  1.6 0.2 shard_map.137
  1.8 0.0 copy-start
  1.8 0.0 copy-start.1
  1.8 0.0 copy-start.6
  1.9 35.1 %all_to_all.15 = f32[64,9,1,128]{3,2,1,0:T(1,128)S(1)} all-to-all(f32[64,9,1,128]{3,2,1,0:T(1,128)S(1)} %bitcast.7), channel_id=1, replica_groups={{344,0,8,16,24,32,40,48,56,64,72,80,88,96,104,112,120,128,136,144,152,1..., dimensions={0} | all-to-all | bytes 589824 | tf_op jit(solution)/shard_map/all_to_all | solution.py:263
  36.9 0.0 copy-done.7
  36.9 0.0 copy-done.8
  36.9 0.0 copy-done.1
  36.9 0.0 copy-done.6
  37.0 1.1 %shard_map.138 = (f32[512,256]{1,0:T(8,128)S(1)}, f32[8,16,128]{2,1,0:T(8,128)S(1)}) custom-call(f32[576,128]{1,0:T(8,128)S(1)} %bitcast.9, bf16[128,192]{1,0:T(8,128)(2,1)S(1)} %copy-done.7, f32[64,256]{1,0:T(8,128)S(1)} %copy-done.6, bf16[2,256,256]{2,1,0:T(8,128)(2,1)S(1)} %copy-done.1, bf16[2,256,256]{2,1,0:T(8,128)(2,1)S(1)} %copy-done, ...), custom_call_target="tpu_custom_call" | custom-call | tf_op jit(solution)/shard_map/pallas_call | solution.py:275
  38.0 7.7 %all_to_all.16.side_ref = f32[8,16,128]{2,1,0:T(8,128)S(1)} all-to-all(f32[8,16,128]{2,1,0:T(8,128)S(1)} %get-tuple-element.13), channel_id=1, replica_groups={{5,6,7,0,1,2,3,4},{13,14,15,8,9,10,11,12},{21,22,23,16,17,18,19,20},{29..., dimensions={0} | all-to-all | bytes 131072 | tf_op jit(solution)/shard_map/all_to_all | solution.py:282
  45.7 1.2 %shard_map.139 = f32[576,128]{1,0:T(8,128)S(1)} custom-call(f32[512,256]{1,0:T(8,128)S(1)} %get-tuple-element.12.spec_ref, f32[8,16,128]{2,1,0:T(8,128)S(1)} %all_to_all.16.side_ref, bf16[128,192]{1,0:T(8,128)(2,1)S(1)} %copy-done.7, f32[64,256]{1,0:T(8,128)S(1)} %copy-done.6, bf16[2,256,256]{2,1,0:T(8,128)(2,1)S(1)} %copy-done.1, ...), custom_call_target="tpu_custom_call" | custom-call | tf_op jit(solution)/shard_map/pallas_call | solution.py:285
  46.9 0.0 copy-start.2
  46.9 0.0 copy-start.3
  46.9 0.0 copy-start.4
  46.9 0.0 copy-start.5
  46.9 28.8 %all_to_all.17 = f32[64,9,1,128]{3,2,1,0:T(1,128)S(1)} all-to-all(f32[64,9,1,128]{3,2,1,0:T(1,128)S(1)} %bitcast.8), channel_id=1, replica_groups={{344,0,8,16,24,32,40,48,56,64,72,80,88,96,104,112,120,128,136,144,152,1..., dimensions={0} | all-to-all | bytes 589824 | tf_op jit(solution)/shard_map/all_to_all | solution.py:263
  75.7 0.0 copy-done.3
  75.7 0.8 %shard_map.140 = (bf16[256,128]{1,0:T(8,128)(2,1)}, bf16[256,128]{1,0:T(8,128)(2,1)}, bf16[256,128]{1,0:T(8,128)(2,1)}, bf16[256,128]{1,0:T(8,128)(2,1)}, f32[16,128]{1,0:T(8,128)}) custom-call(f32[576,128]{1,0:T(8,128)S(1)} %bitcast.6, bf16[256,128]{1,0:T(8,128)(2,1)S(1)} %copy-done.2, bf16[256,128]{1,0:T(8,128)(2,1)S(1)} %copy-done.5, ...), custom_call_target="tpu_custom_call" | custom-call | tf_op jit(solution)/shard_map/pallas_call | solution.py:290
  (4 shorter events, 0.0 us)
Async XLA Ops:
  0.6 1.0 %copy-start.9 = (f32[128,16]{0,1:T(8,128)S(1)}, f32[128,16]{0,1:T(8,128)}, u32[]{:S(2)}) copy-start(f32[128,16]{0,1:T(8,128)} %param.13) | copy-start | bytes 24580
  1.6 35.3 %copy-start.7 = (bf16[128,192]{1,0:T(8,128)(2,1)S(1)}, bf16[128,192]{1,0:T(8,128)(2,1)}, u32[]{:S(2)}) copy-start(bf16[128,192]{1,0:T(8,128)(2,1)} %constant.10.clone.first_ref) | copy-start | bytes 147460
  1.6 35.3 %copy-start.8 = (bf16[64,384]{1,0:T(8,128)(2,1)S(1)}, bf16[64,384]{1,0:T(8,128)(2,1)}, u32[]{:S(2)}) copy-start(bf16[64,384]{1,0:T(8,128)(2,1)} %constant.14.clone.last_ref) | copy-start | bytes 147460
  1.8 35.1 %copy-start = (bf16[2,256,256]{2,1,0:T(8,128)(2,1)S(1)}, bf16[2,256,256]{2,1,0:T(8,128)(2,1)}, u32[]{:S(2)}) copy-start(bf16[2,256,256]{2,1,0:T(8,128)(2,1)} %constant.13.clone.inverse_ref) | copy-start | bytes 786436
  1.8 35.1 %copy-start.1 = (bf16[2,256,256]{2,1,0:T(8,128)(2,1)S(1)}, bf16[2,256,256]{2,1,0:T(8,128)(2,1)}, u32[]{:S(2)}) copy-start(bf16[2,256,256]{2,1,0:T(8,128)(2,1)} %constant.12.clone.forward_ref) | copy-start | bytes 786436
  1.8 35.1 %copy-start.6 = (f32[64,256]{1,0:T(8,128)S(1)}, f32[64,256]{1,0:T(8,128)}, u32[]{:S(2)}) copy-start(f32[64,256]{1,0:T(8,128)} %constant.11.clone.twiddle_ref) | copy-start | bytes 196612
  46.9 28.8 %copy-start.2 = (bf16[256,128]{1,0:T(8,128)(2,1)S(1)}, bf16[256,128]{1,0:T(8,128)(2,1)}, u32[]{:S(2)}) copy-start(bf16[256,128]{1,0:T(8,128)(2,1)} %query_ref.1) | copy-start | bytes 196612
  46.9 28.8 %copy-start.3 = (bf16[256,128]{1,0:T(8,128)(2,1)S(1)}, bf16[256,128]{1,0:T(8,128)(2,1)}, u32[]{:S(2)}) copy-start(bf16[256,128]{1,0:T(8,128)(2,1)} %upstream_ref.1) | copy-start | bytes 196612
  46.9 28.8 %copy-start.4 = (bf16[256,128]{1,0:T(8,128)(2,1)S(1)}, bf16[256,128]{1,0:T(8,128)(2,1)}, u32[]{:S(2)}) copy-start(bf16[256,128]{1,0:T(8,128)(2,1)} %value_ref.1) | copy-start | bytes 196612
  46.9 28.8 %copy-start.5 = (bf16[256,128]{1,0:T(8,128)(2,1)S(1)}, bf16[256,128]{1,0:T(8,128)(2,1)}, u32[]{:S(2)}) copy-start(bf16[256,128]{1,0:T(8,128)(2,1)} %key_ref.1) | copy-start | bytes 196612
